TPU v7x, 32 devices: a whole 2x2x4 slice. The times are simulated.
32 devices in a mesh: dp: 4 (over y, x), fsdp: 8 (over z, core).
Axes of the slice: x: 2, y: 2, z: 4, core: 2. Of those that a mesh axis runs over, the one named last changes fastest.
Arguments:
- tokens: bfloat16 [64, 197, 768], P(('dp', 'fsdp')), may hold values from -6 to 6
- counts: int32 [64], P(('dp', 'fsdp')), may hold values from 65 to 197, as said below
- params_first: bfloat16 [7098368], P(('dp', 'fsdp')), may hold values from -3 to 3
- params_second: bfloat16 [7098368], P(('dp', 'fsdp')), may hold values from -3 to 3
- cotangent: bfloat16 [64, 197, 768], P(('dp', 'fsdp')), may hold values from -6 to 6
Outputs:
- output: bfloat16 [64, 197, 768], P(('dp', 'fsdp'))
- grad_tokens: bfloat16 [64, 197, 768], P(('dp', 'fsdp'))
- grad_first: float32 [7098368], P(('dp', 'fsdp'))
- grad_second: float32 [7098368], P(('dp', 'fsdp'))
Inputs may be any that keep to these rules, and one draw needn't show every extreme that they name: Keys 0 to counts - 1 of an image are valid; some image has all 197.
All inputs are finite; a program needn't handle non-finite values.
Results may differ from a plain program's by a relative error of at most 0.015.
Values may be sent and summed in bfloat16 or wider, within the bound.
No kernel may reach another device: no remote copies, remote signals or barrier semaphores. Data moves between devices by JAX's collectives and lax.ppermute only.
A program may use at most 256 MiB of HBM per device.

v0:
```python
import math

import jax
import jax.numpy as jnp
from jax import lax
from jax.sharding import PartitionSpec as P

D = 768
HEADS = 12
FF = 3072
GRID = 14
SEQ = 197
RELS = 732


EPSILON = 1e-06
NEGATIVE = -1000000000.0


def param_layout():
    return [
        ("norm1_gain", (D,)),
        ("norm1_bias", (D,)),
        ("qkv_weight", (D, 3 * D)),
        ("query_bias", (D,)),
        ("value_bias", (D,)),
        ("relative_table", (RELS, HEADS)),
        ("proj_weight", (D, D)),
        ("proj_bias", (D,)),
        ("gamma_attn", (D,)),
        ("norm2_gain", (D,)),
        ("norm2_bias", (D,)),
        ("fc1_weight", (D, FF)),
        ("fc1_bias", (FF,)),
        ("fc2_weight", (FF, D)),
        ("fc2_bias", (D,)),
        ("gamma_mlp", (D,)),
    ]


def unpack_layer(flat):
    pieces = {}
    offset = 0
    for entry_name, dims_shape in param_layout():
        length = math.prod(dims_shape)
        pieces[entry_name] = flat[offset : offset + length].reshape(dims_shape)
        offset += length
    return pieces


def relative_index():
    patches = GRID * GRID
    position = jnp.arange(patches, dtype=jnp.int32)
    row_pos = position // GRID
    col_pos = position % GRID
    delta_row = row_pos[:, None] - row_pos[None, :] + (GRID - 1)
    delta_col = col_pos[:, None] - col_pos[None, :] + (GRID - 1)
    inner_index = delta_row * (2 * GRID - 1) + delta_col
    top_row = jnp.full((1, patches), RELS - 3, jnp.int32)
    left_col = jnp.full((patches, 1), RELS - 2, jnp.int32)
    corner = jnp.full((1, 1), RELS - 1, jnp.int32)
    upper = jnp.concatenate([corner, top_row], axis=1)
    lower = jnp.concatenate([left_col, inner_index], axis=1)
    return jnp.concatenate([upper, lower], axis=0)


def norm_apply(values, gain, shift):
    centre = values - jnp.mean(values, axis=-1, keepdims=True)
    spread = jnp.mean(centre * centre, axis=-1, keepdims=True)
    return centre * lax.rsqrt(spread + EPSILON) * gain + shift


def softmax_rows(scores):
    shifted = jnp.exp(scores - jnp.max(scores, axis=-1, keepdims=True))
    return shifted / jnp.sum(shifted, axis=-1, keepdims=True)


def gelu_exact(values):
    return jax.nn.gelu(values, approximate=False)


def as_float(params, entry_name):
    return params[entry_name].astype(jnp.float32)


def layer_forward(hidden, valid, params):
    images = hidden.shape[0]
    head_dim = D // HEADS
    factor = head_dim ** (-0.5)
    token_rows = hidden.reshape(-1, D)
    normed = norm_apply(token_rows, as_float(params, "norm1_gain"), as_float(params, "norm1_bias"))
    normed_low = normed.astype(jnp.bfloat16)
    project = jnp.dot(normed_low, params["qkv_weight"], preferred_element_type=jnp.float32)
    query_low = ((project[:, :D] + as_float(params, "query_bias")) * factor).astype(jnp.bfloat16)
    query_low = query_low.reshape(images, SEQ, HEADS, head_dim)
    key_low = project[:, D : 2 * D].astype(jnp.bfloat16).reshape(images, SEQ, HEADS, head_dim)
    value_low = (project[:, 2 * D :] + as_float(params, "value_bias")).astype(jnp.bfloat16)
    value_low = value_low.reshape(images, SEQ, HEADS, head_dim)
    index_table = relative_index()
    table = jnp.take(as_float(params, "relative_table"), index_table.reshape(-1), axis=0)
    table = table.reshape(SEQ, SEQ, HEADS).transpose(2, 0, 1)
    visible = jnp.arange(SEQ)[None, :] < valid[:, None]
    raw_scores = jnp.einsum(
        "bqhd,bkhd->bhqk", query_low, key_low, preferred_element_type=jnp.float32
    )
    scores = jnp.where(visible[:, None, None, :], raw_scores + table[None], NEGATIVE)
    weights = softmax_rows(scores)
    weights_low = weights.astype(jnp.bfloat16)
    attended_low = (
        jnp.einsum("bhqk,bkhd->bqhd", weights_low, value_low, preferred_element_type=jnp.float32)
        .reshape(-1, D)
        .astype(jnp.bfloat16)
    )
    branch = jnp.dot(attended_low, params["proj_weight"], preferred_element_type=jnp.float32)
    branch = branch + as_float(params, "proj_bias")
    middle = token_rows + as_float(params, "gamma_attn") * branch
    second_low = norm_apply(
        middle, as_float(params, "norm2_gain"), as_float(params, "norm2_bias")
    ).astype(jnp.bfloat16)
    pre_act = jnp.dot(second_low, params["fc1_weight"], preferred_element_type=jnp.float32)
    pre_act = pre_act + as_float(params, "fc1_bias")
    activ_low = gelu_exact(pre_act).astype(jnp.bfloat16)
    mlp_out = jnp.dot(activ_low, params["fc2_weight"], preferred_element_type=jnp.float32)
    mlp_out = mlp_out + as_float(params, "fc2_bias")
    result = middle + as_float(params, "gamma_mlp") * mlp_out
    saved = {
        "token_rows": token_rows,
        "normed_low": normed_low,
        "query_low": query_low,
        "key_low": key_low,
        "value_low": value_low,
        "index_table": index_table,
        "weights": weights,
        "weights_low": weights_low,
        "attended_low": attended_low,
        "branch": branch,
        "middle": middle,
        "second_low": second_low,
        "pre_act": pre_act,
        "activ_low": activ_low,
        "mlp_out": mlp_out,
    }
    return (result.reshape(images, SEQ, D), saved)


def layer_backward(grad_out, params, saved, flat_length):
    images = grad_out.shape[0]
    head_dim = D // HEADS
    factor = head_dim ** (-0.5)
    grad_rows = grad_out.reshape(-1, D)
    grads = {}
    grads["gamma_mlp"] = jnp.sum(grad_rows * saved["mlp_out"], axis=0)
    grad_mlp = grad_rows * as_float(params, "gamma_mlp")
    grads["fc2_bias"] = jnp.sum(grad_mlp, axis=0)
    grad_mlp_low = grad_mlp.astype(jnp.bfloat16)
    grads["fc2_weight"] = jnp.dot(
        saved["activ_low"].T, grad_mlp_low, preferred_element_type=jnp.float32
    )
    grad_activ = jnp.dot(grad_mlp_low, params["fc2_weight"].T, preferred_element_type=jnp.float32)
    gelu_pull = jax.vjp(gelu_exact, saved["pre_act"])[1]
    grad_pre = gelu_pull(grad_activ)[0]
    grads["fc1_bias"] = jnp.sum(grad_pre, axis=0)
    grad_pre_low = grad_pre.astype(jnp.bfloat16)
    grads["fc1_weight"] = jnp.dot(
        saved["second_low"].T, grad_pre_low, preferred_element_type=jnp.float32
    )
    grad_second = jnp.dot(grad_pre_low, params["fc1_weight"].T, preferred_element_type=jnp.float32)
    second_pull = jax.vjp(
        norm_apply, saved["middle"], as_float(params, "norm2_gain"), as_float(params, "norm2_bias")
    )[1]
    grad_mid_norm, grads["norm2_gain"], grads["norm2_bias"] = second_pull(grad_second)
    grad_middle = grad_rows + grad_mid_norm
    grads["gamma_attn"] = jnp.sum(grad_middle * saved["branch"], axis=0)
    grad_branch = grad_middle * as_float(params, "gamma_attn")
    grads["proj_bias"] = jnp.sum(grad_branch, axis=0)
    grad_branch_low = grad_branch.astype(jnp.bfloat16)
    grads["proj_weight"] = jnp.dot(
        saved["attended_low"].T, grad_branch_low, preferred_element_type=jnp.float32
    )
    grad_attended = jnp.dot(
        grad_branch_low, params["proj_weight"].T, preferred_element_type=jnp.float32
    )
    grad_attended_low = grad_attended.astype(jnp.bfloat16).reshape(images, SEQ, HEADS, head_dim)
    grad_weights = jnp.einsum(
        "bqhd,bkhd->bhqk", grad_attended_low, saved["value_low"], preferred_element_type=jnp.float32
    )
    grad_value = jnp.einsum(
        "bhqk,bqhd->bkhd",
        saved["weights_low"],
        grad_attended_low,
        preferred_element_type=jnp.float32,
    ).reshape(-1, D)
    weights = saved["weights"]
    grad_scores = weights * (grad_weights - jnp.sum(weights * grad_weights, axis=-1, keepdims=True))
    grad_table = jnp.sum(grad_scores, axis=0).transpose(1, 2, 0).reshape(SEQ * SEQ, HEADS)
    grads["relative_table"] = jax.ops.segment_sum(
        grad_table, saved["index_table"].reshape(-1), num_segments=RELS
    )
    grad_scores_low = grad_scores.astype(jnp.bfloat16)
    grad_query = (
        jnp.einsum(
            "bhqk,bkhd->bqhd", grad_scores_low, saved["key_low"], preferred_element_type=jnp.float32
        ).reshape(-1, D)
        * factor
    )
    grad_key = jnp.einsum(
        "bhqk,bqhd->bkhd", grad_scores_low, saved["query_low"], preferred_element_type=jnp.float32
    ).reshape(-1, D)
    grads["query_bias"] = jnp.sum(grad_query, axis=0)
    grads["value_bias"] = jnp.sum(grad_value, axis=0)
    grad_project_low = jnp.concatenate([grad_query, grad_key, grad_value], axis=1).astype(
        jnp.bfloat16
    )
    grads["qkv_weight"] = jnp.dot(
        saved["normed_low"].T, grad_project_low, preferred_element_type=jnp.float32
    )
    grad_normed = jnp.dot(
        grad_project_low, params["qkv_weight"].T, preferred_element_type=jnp.float32
    )
    first_pull = jax.vjp(
        norm_apply,
        saved["token_rows"],
        as_float(params, "norm1_gain"),
        as_float(params, "norm1_bias"),
    )[1]
    grad_rows_norm, grads["norm1_gain"], grads["norm1_bias"] = first_pull(grad_normed)
    grad_hidden = grad_middle + grad_rows_norm
    pieces = [grads[entry_name].reshape(-1) for entry_name, dims_shape in param_layout()]
    used = sum((piece.shape[0] for piece in pieces))
    pieces.append(jnp.zeros((flat_length - used,), jnp.float32))
    return (grad_hidden.reshape(images, SEQ, D), jnp.concatenate(pieces))


def local(tokens, counts, params_first, params_second, cotangent):
    shards = (params_first, params_second)
    gathered = [
        lax.all_gather(shard_piece, ("dp", "fsdp"), axis=0, tiled=True) for shard_piece in shards
    ]
    hidden = tokens.astype(jnp.float32)
    layer_inputs = []
    for layer_number in range(2):
        layer_inputs.append(hidden)
        hidden, unused = layer_forward(hidden, counts, unpack_layer(gathered[layer_number]))
    output = hidden.astype(jnp.bfloat16)
    grad_hidden = cotangent.astype(jnp.float32)
    grad_shards = [None, None]
    for layer_number in (1, 0):
        flat = lax.all_gather(shards[layer_number], ("dp", "fsdp"), axis=0, tiled=True)
        params = unpack_layer(flat)
        unused, saved = layer_forward(layer_inputs[layer_number], counts, params)
        grad_hidden, grad_flat = layer_backward(grad_hidden, params, saved, flat.shape[0])

        def grad_rows(start, count, grad_flat=grad_flat):
            return grad_flat

        grad_shards[layer_number] = lax.psum_scatter(
            grad_rows(jnp.int32(0), shards[layer_number].shape[0] * lax.axis_size(("dp", "fsdp"))),
            ("dp", "fsdp"),
            scatter_dimension=0,
            tiled=True,
        )
    return (output, grad_hidden.astype(jnp.bfloat16), grad_shards[0], grad_shards[1])


def solution(mesh):
    return jax.shard_map(
        local,
        mesh=mesh,
        in_specs=(
            P(("dp", "fsdp"), None, None),
            P(("dp", "fsdp")),
            P(("dp", "fsdp")),
            P(("dp", "fsdp")),
            P(("dp", "fsdp"), None, None),
        ),
        out_specs=(
            P(("dp", "fsdp"), None, None),
            P(("dp", "fsdp"), None, None),
            P(("dp", "fsdp")),
            P(("dp", "fsdp")),
        ),
        check_vma=False,
    )
```

profile of v0, /device:TPU:11, one launch (start us, length us, event | category | flops | bytes accessed | tf_op | source)
XLA Modules:
  0.0 3335.2 jit_solution(10155045354360449117)
XLA Ops:
  30.2 152.8 %all-gather.5.cloned.1.call-done = bf16[32,1,221824]{2,1,0:T(2,128)(2,1)} async-done(((bf16[1,1,221824]{2,1,0:T(2,128)(2,1)}), bf16[32,1,221824]{2,1,0:T(2,128)(2,1)}) %all-gather.5.cloned.1.call-update) | async-done | bytes 14196752 | tf_op jit(solution)/shard_map/all_gather | solution.py:237
  183.0 301.1 %reduce.9 = bf16[32,221824]{1,0:T(8,128)(2,1)} reduce(bf16[32,1,221824]{2,1,0:T(2,128)(2,1)} %all-gather.5.cloned.1.call-done, bf16[]{:T(256)} %constant.157), dimensions={1}, to_apply=%all-gather.reduce_sub_computation | reduce | bytes 28393474 | tf_op jit(solution)/shard_map/all_gather | solution.py:237
  484.2 25.3 reshape.510
  509.5 10.9 fusion.90
  530.0 300.9 %reduce.10 = bf16[32,221824]{1,0:T(8,128)(2,1)} reduce(bf16[32,1,221824]{2,1,0:T(2,128)(2,1)} %all-gather.7.cloned.1.call-done, bf16[]{:T(256)} %constant.157), dimensions={1}, to_apply=%all-gather.1.reduce_sub_computation | reduce | bytes 28393474 | tf_op jit(solution)/shard_map/all_gather | solution.py:237
  830.9 25.2 reshape.512
  865.5 10.9 fusion.89
  896.0 128.8 %gather_fusion.1 = f32[38809,12]{1,0:T(8,128)} fusion(f32[732,12]{1,0:T(8,128)S(1)} %reshape.472, s32[38912]{0:T(1024)S(1)} %copy-done.46), kind=kCustom, calls=%fused_computation.1.clone | custom fusion | bytes 3880900 | tf_op jit(solution)/shard_map/jit(_take)/gather | solution.py:100
  1024.8 129.4 %gather_fusion = f32[38809,12]{1,0:T(8,128)} fusion(f32[732,12]{1,0:T(8,128)S(1)} %reshape.471, s32[38912]{0:T(1024)S(1)} %copy-done.46), kind=kCustom, calls=%fused_computation.clone | custom fusion | bytes 3880900 | tf_op jit(solution)/shard_map/jit(_take)/gather | solution.py:100
  1154.2 26.8 broadcast_select_fusion
  1181.0 11.1 copy.212
  1242.8 16.3 multiply_convert_fusion.1
  1272.4 12.1 copy.222
  1348.2 15.9 fusion.79
  1531.8 11.0 copy.254
  1542.8 207.7 %scatter_custom_fusion = f32[732,12]{1,0:T(8,128)S(1)} fusion(s32[38809]{0:T(1024)} %copy-done.47, f32[38809,12]{1,0:T(8,128)} %copy.254, f32[]{:T(128)} %constant.45.clone.1), kind=kCustom, calls=%fused_computation.174 | custom fusion | flops 465708 | bytes 35648 | tf_op jit(solution)/shard_map/scatter-add | solution.py:196
  1763.6 10.7 reshape.464
  1789.8 11.0 copy.256
  1800.7 207.7 %scatter_custom_fusion.1 = f32[732,12]{1,0:T(8,128)S(1)} fusion(s32[38809]{0:T(1024)} %copy-done.47, f32[38809,12]{1,0:T(8,128)} %copy.256, f32[]{:T(128)} %constant.45.clone.1), kind=kCustom, calls=%fused_computation.172 | custom fusion | flops 465708 | bytes 35648 | tf_op jit(solution)/shard_map/scatter-add | solution.py:196
  2012.2 9.5 copy.284
  2021.8 10.8 reshape.470
  2032.6 242.0 %concatenate.30 = f32[7098368]{0:T(1024)} concatenate(f32[768]{0:T(1024)S(1)} %get-tuple-element.31, f32[768]{0:T(1024)S(1)} %get-tuple-element.42, f32[1769472]{0:T(1024)} %reshape.459, f32[768]{0:T(1024)S(1)} %reduce_sum.440, f32[768]{0:T(1024)S(1)} %reduce_sum.442, f32[8784]{0:T(1024)S(1)} %reshape.461, f32[589824]{0:T(1024)} %reshape.462, f32[768]{0:T(1024)S(1)} %get-tuple-element.41, ...), dimensions={0} | concatenate | bytes 56786944 | tf_op jit(solution)/shard_map/concatenate | solution.py:231
  2274.6 241.9 %concatenate.31 = f32[7098368]{0:T(1024)} concatenate(f32[768]{0:T(1024)S(1)} %get-tuple-element.27, f32[768]{0:T(1024)S(1)} %get-tuple-element.36, f32[1769472]{0:T(1024)} %reshape.465, f32[768]{0:T(1024)S(1)} %reduce_sum.463, f32[768]{0:T(1024)S(1)} %reduce_sum.468, f32[8784]{0:T(1024)S(1)} %reshape.467, f32[589824]{0:T(1024)} %reshape.468, f32[768]{0:T(1024)S(1)} %copy-done.78, ...), dimensions={0} | concatenate | bytes 56786944 | tf_op jit(solution)/shard_map/concatenate | solution.py:231
  2522.5 800.8 %all-reduce.6.cloned.1.call-done = (f32[7098368]{0:T(1024)}, f32[7098368]{0:T(1024)}) async-done(((f32[7098368]{0:T(1024)}, f32[7098368]{0:T(1024)}), (f32[7098368]{0:T(1024)}, f32[7098368]{0:T(1024)})) %all-reduce.6.cloned.1.call-update) | async-done | bytes 56786960
  (426 shorter events, 398.9 us)
Async XLA Ops:
  7.2 175.8 %all-gather.5.cloned.1.call-start = ((), (), s32[]{:S(2)}) async-start(), calls=%async_computation | async-start | bytes 29280768 | tf_op jit(solution)/shard_map/all_gather | solution.py:237
  13.2 516.8 %all-gather.7.cloned.1.call-start = ((), (), s32[]{:S(2)}) async-start(), calls=%async_computation.1 | async-start | bytes 29280768 | tf_op jit(solution)/shard_map/all_gather | solution.py:237
  19.1 3304.3 %all-reduce.6.cloned.1.call-start = ((), (), s32[]{:S(2)}) async-start(), calls=%async_computation.2 | async-start | bytes 113573888
  29.6 454.6 %copy-start.67 = (f32[394]{0:T(512)}, f32[394]{0:T(512)S(1)}, u32[]{:S(2)}) copy-start(f32[394]{0:T(512)S(1)} %add.385) | copy-start | bytes 4732
  528.6 349.2 %copy-start.61 = (f32[768]{0:T(1024)}, f32[768]{0:T(1024)S(1)}, u32[]{:S(2)}) copy-start(f32[768]{0:T(1024)S(1)} %get-tuple-element.87) | copy-start | bytes 9220
  528.6 349.2 %copy-start.71 = (f32[768]{0:T(1024)}, f32[768]{0:T(1024)S(1)}, u32[]{:S(2)}) copy-start(f32[768]{0:T(1024)S(1)} %get-tuple-element.86) | copy-start | bytes 9220
  1024.8 129.4 %copy-start.54 = (pred[38809]{0:T(1024)(128)(4,1)S(1)}, pred[38809]{0:T(1024)(128)(4,1)}, u32[]{:S(2)}) copy-start(pred[38809]{0:T(1024)(128)(4,1)} %compare_and_fusion) | copy-start | bytes 116431
  1242.8 16.3 copy-start.5
  1242.8 16.3 copy-start.28
  1242.8 16.3 copy-start.79
  1242.8 16.3 copy-start.97
  1262.4 57.4 %copy-start.7 = (f32[394,768]{1,0:T(8,128)}, f32[394,768]{1,0:T(8,128)S(1)}, u32[]{:S(2)}) copy-start(f32[394,768]{1,0:T(8,128)S(1)} %get-tuple-element.62) | copy-start | bytes 3631108
  1296.2 12.6 copy-start.36
  1343.5 20.6 slice-start.6
  1348.2 16.0 slice-start.7
  1379.8 12.4 slice-start.2
  1439.3 12.4 slice-start
  2032.5 242.0 %copy-start.69 = (f32[768]{0:T(1024)S(1)}, f32[768]{0:T(1024)}, u32[]{:S(2)}) copy-start(f32[768]{0:T(1024)} %get-tuple-element.107) | copy-start | bytes 9220
  2032.5 242.0 %copy-start.77 = (f32[768]{0:T(1024)S(1)}, f32[768]{0:T(1024)}, u32[]{:S(2)}) copy-start(f32[768]{0:T(1024)} %get-tuple-element.34) | copy-start | bytes 9220
  2032.5 242.0 %copy-start.78 = (f32[768]{0:T(1024)S(1)}, f32[768]{0:T(1024)}, u32[]{:S(2)}) copy-start(f32[768]{0:T(1024)} %get-tuple-element.35) | copy-start | bytes 9220
  2032.5 242.0 %copy-start.82 = (f32[3072]{0:T(1024)S(1)}, f32[3072]{0:T(1024)}, u32[]{:S(2)}) copy-start(f32[3072]{0:T(1024)} %get-tuple-element.45) | copy-start | bytes 36868
  2032.5 242.0 %copy-start.86 = (f32[768]{0:T(1024)S(1)}, f32[768]{0:T(1024)}, u32[]{:S(2)}) copy-start(f32[768]{0:T(1024)} %get-tuple-element.25) | copy-start | bytes 9220
  2032.5 242.0 %copy-start.87 = (f32[768]{0:T(1024)S(1)}, f32[768]{0:T(1024)}, u32[]{:S(2)}) copy-start(f32[768]{0:T(1024)} %get-tuple-element.33) | copy-start | bytes 9220
  2032.5 242.0 %copy-start.88 = (f32[768]{0:T(1024)S(1)}, f32[768]{0:T(1024)}, u32[]{:S(2)}) copy-start(f32[768]{0:T(1024)} %get-tuple-element.103) | copy-start | bytes 9220
  (96 other events, 491.0 us)
Sparse Core Ops, SparseCore 0:
  13.3 169.6 all-gather.4
  186.5 168.2 all-gather.6
  2516.6 806.6 all-reduce.5
where the time goes:
time: 3380 us; the launch traced here: 3340 us
  local copies, waits for them, and re-layouts  1130 us (33%)
  other arithmetic  1080 us (32%)
  waiting for transfers between devices  954 us (28%)
  matrix products  153 us (5%)
    unnamed x4, waiting for transfers between devices  801 us
    all_gather x2, other arithmetic, local(): lax.all_gather(shard_piece, ('dp', 'fsdp'), axis=0, tiled=True)  602 us
    concatenate x2, local copies, waits for them, and re-layouts, layer_backward(): return (grad_hidden.reshape(images, SEQ, D), jnp.concatenate(pieces))  484 us
    scatter-add x2, other arithmetic, layer_backward(): jax.ops.segment_sum(grad_table, saved['index_table'].reshape(-1), num_seg...  415 us
    gather x2, local copies, waits for them, and re-layouts, layer_forward(): jnp.take(as_float(params, 'relative_table'), index_table.reshape(-1), axi...  258 us
    all_gather x2, waiting for transfers between devices, local(): lax.all_gather(shard_piece, ('dp', 'fsdp'), axis=0, tiled=True)  153 us
    unnamed x249, local copies, waits for them, and re-layouts  104 us
  transfers between devices with their start and end apart: 3, of which 2 were waited for; matrix products, arithmetic and copies ran while one was open for 11% of the time, Pallas kernels for 0%

commit v1 on v0

v1 whole, which is shorter than its diff:
```python
import functools
import math

import jax
import jax.numpy as jnp
import numpy as np
from jax import lax
from jax.experimental import pallas as pl
from jax.experimental.pallas import tpu as pltpu
from jax.sharding import PartitionSpec as P

D = 768
HEADS = 12
HEAD = D // HEADS
FF = 3072
GRID = 14
SEQ = 197
RELS = 732
ROWS = 208
LANES = 128
TILE = 16
AXES = ("dp", "fsdp")
VMEM_LIMIT = 56 * 2**20

EPSILON = 1e-06
NEGATIVE = -1000000000.0

ENTRIES = [
    ("norm1_gain", (D,)),
    ("norm1_bias", (D,)),
    ("qkv_weight", (D, 3 * D)),
    ("query_bias", (D,)),
    ("value_bias", (D,)),
    ("relative_table", (RELS, HEADS)),
    ("proj_weight", (D, D)),
    ("proj_bias", (D,)),
    ("gamma_attn", (D,)),
    ("norm2_gain", (D,)),
    ("norm2_bias", (D,)),
    ("fc1_weight", (D, FF)),
    ("fc1_bias", (FF,)),
    ("fc2_weight", (FF, D)),
    ("fc2_bias", (D,)),
    ("gamma_mlp", (D,)),
]
WEIGHTS = {name: dims for name, dims in ENTRIES if name.endswith("weight")}
SIZES = dict(ENTRIES)
VECTORS = [
    "norm1_gain",
    "norm1_bias",
    "query_bias",
    "value_bias",
    "proj_bias",
    "gamma_attn",
    "norm2_gain",
    "norm2_bias",
    "fc2_bias",
    "gamma_mlp",
]
ROW = {name: i for i, name in enumerate(VECTORS)}


def count_rows(dims):
    return -(-math.prod(dims) // LANES)


def virtual_starts():
    starts, at = {}, 0
    for name, dims in ENTRIES:
        starts[name] = at
        at += count_rows(dims)
    return starts, at


STARTS, VIRTUAL = virtual_starts()
SHIFT = RELS * HEADS % LANES
TABLE_END = STARTS["proj_weight"]


def tile_order():
    parts = []
    for name, (depth, width) in WEIGHTS.items():
        across = width // LANES
        rows = STARTS[name] + np.arange(depth * across).reshape(depth // TILE, TILE, across)
        parts.append(rows.transpose(0, 2, 1).reshape(-1))
    return np.concatenate(parts)


def small_order():
    groups = [VECTORS, ["fc1_bias"], ["relative_table"]]
    rows = []
    for group in groups:
        for name in group:
            rows += [STARTS[name] + i for i in range(count_rows(SIZES[name]))]
        rows += [-1] * (-len(rows) % 8)
    return np.array(rows)


TILE_ROWS = tile_order()
SMALL_ROWS = small_order()
TILES = len(TILE_ROWS) // TILE


def halo(block, before, after, devices):
    rows = block.shape[0]
    pieces = [block]
    for hop in range(1, -(-before // rows) + 1):
        take = min(rows, before - (hop - 1) * rows)
        perm = [(i, i + hop) for i in range(devices - hop)]
        pieces.insert(0, lax.ppermute(block[rows - take :], AXES, perm))
    for hop in range(1, -(-after // rows) + 1):
        take = min(rows, after - (hop - 1) * rows)
        perm = [(i + hop, i) for i in range(devices - hop)]
        pieces.append(lax.ppermute(block[:take], AXES, perm))
    return jnp.concatenate(pieces, axis=0)


def pick_rows(index, source):
    chosen = index[:, None] == lax.broadcasted_iota(jnp.int32, (1, source.shape[0]), 1)
    chosen = chosen.astype(jnp.bfloat16)
    if source.dtype == jnp.bfloat16:
        return jnp.dot(chosen, source, preferred_element_type=jnp.float32).astype(jnp.bfloat16)
    high = source.astype(jnp.bfloat16)
    low = (source - high.astype(jnp.float32)).astype(jnp.bfloat16)
    return jnp.dot(chosen, high, preferred_element_type=jnp.float32) + jnp.dot(
        chosen, low, preferred_element_type=jnp.float32
    )


def round_up(value, unit):
    return -(-value // unit) * unit


def owned_rows(flat, me, devices):
    length = flat.shape[0] // LANES
    share = len(TILE_ROWS) // devices
    wanted = TILE_ROWS.reshape(devices, share) - np.arange(devices)[:, None] * length
    before = round_up(max(0, -wanted.min()) + 1, TILE)
    after = round_up(max(0, wanted.max() + 1 - length), TILE)
    wanted = wanted + before - 1
    smalls = SMALL_ROWS[None] - np.arange(devices)[:, None] * length
    smalls = np.where((smalls >= 0) & (smalls < length), smalls + before - 1, -1)
    index = jnp.asarray(np.concatenate([wanted, smalls], axis=1).astype(np.int32))
    around = halo(flat.reshape(length, LANES), before, after, devices)
    shifted = jnp.concatenate([around[:-1, SHIFT:], around[1:, :SHIFT]], axis=1)
    at = me * length - before + 1 + lax.broadcasted_iota(jnp.int32, (shifted.shape[0], 1), 0)
    virtual = jnp.where(at < TABLE_END, around[1:], shifted)
    picked = pick_rows(lax.dynamic_index_in_dim(index, me, 0, keepdims=False), virtual)
    return picked[:share], picked[share:]


def flat_share(owned, smalls, me, devices, flat_length):
    length = flat_length // LANES // devices
    share = len(TILE_ROWS) // devices
    place = np.full(max(VIRTUAL, devices * length + 1), -1, np.int64)
    place[TILE_ROWS] = np.arange(len(TILE_ROWS))
    small_place = np.full(place.shape, -1, np.int64)
    small_place[SMALL_ROWS[SMALL_ROWS >= 0]] = np.flatnonzero(SMALL_ROWS >= 0)
    span = np.arange(devices)[:, None] * length + np.arange(length + 1)[None]
    relative = place[span] - np.arange(devices)[:, None] * share
    has = place[span] >= 0
    before = round_up(max(0, -relative[has].min()), TILE)
    after = round_up(max(0, relative[has].max() + 1 - share), TILE)
    smalls_at = before + share + after
    index = np.where(has, relative + before, -1)
    index = np.where(small_place[span] >= 0, small_place[span] + smalls_at, index)
    index = jnp.asarray(index.astype(np.int32))
    source = jnp.concatenate([halo(owned, before, after, devices), smalls], axis=0)
    virtual = pick_rows(lax.dynamic_index_in_dim(index, me, 0, keepdims=False), source)
    here, following = virtual[:-1], virtual[1:]
    at = me * length + lax.broadcasted_iota(jnp.int32, (length, 1), 0)
    lane = lax.broadcasted_iota(jnp.int32, (1, LANES), 1)
    shifted = jnp.concatenate([here[:, LANES - SHIFT :], following[:, : LANES - SHIFT]], axis=1)
    straight = (at < TABLE_END - 1) | ((at == TABLE_END - 1) & (lane < SHIFT))
    return jnp.where(straight, here, shifted).reshape(-1)


VECTOR_ROWS = len(VECTORS) * D // LANES
FC1_AT = round_up(VECTOR_ROWS, 8)
TABLE_AT = FC1_AT + FF // LANES
TABLE_ROWS = count_rows(SIZES["relative_table"])


def unpack_smalls(rows):
    vectors = rows[:, :VECTOR_ROWS].astype(jnp.float32).reshape(2, len(VECTORS), D)
    vectors = jnp.pad(vectors, ((0, 0), (0, 16 - len(VECTORS)), (0, 0)))
    fc1 = rows[:, FC1_AT:TABLE_AT].astype(jnp.float32).reshape(2, 1, FF)
    table = rows[:, TABLE_AT : TABLE_AT + TABLE_ROWS].reshape(2, -1)[:, : RELS * HEADS]
    return vectors, fc1, table.reshape(2, RELS, HEADS)


def pack_smalls(vectors, fc1, table):
    vectors = vectors.reshape(2, VECTOR_ROWS, LANES)
    vectors = jnp.pad(vectors, ((0, 0), (0, FC1_AT - VECTOR_ROWS), (0, 0)))
    table = jnp.pad(table.reshape(2, RELS * HEADS), ((0, 0), (0, round_up(TABLE_ROWS, 8) * LANES - RELS * HEADS)))
    return jnp.concatenate([vectors, fc1.reshape(2, -1, LANES), table.reshape(2, -1, LANES)], axis=1)


def column_choice():
    offset = np.arange(GRID)[:, None] - np.arange(GRID)[None, :] + GRID - 1
    return (np.arange(2 * GRID - 1)[:, None] == offset.reshape(1, -1)).astype(np.float32)


SIDE = 2 * GRID - 1
PATCHES = GRID * GRID
WINDOW = round_up(SIDE * GRID, LANES) + LANES
WIDE = round_up(ROWS, LANES)


def bias_kernel(spread_ref, ends_ref, bias_ref):
    lane = lax.broadcasted_iota(jnp.int32, (1, WIDE), 1)
    inner = (lane >= 1) & (lane < SEQ)
    top, left, corner = ends_ref[0, 0:1, 0:1], ends_ref[0, 1:2, 0:1], ends_ref[0, 2:3, 0:1]
    bias_ref[...] = jnp.zeros_like(bias_ref)
    bias_ref[0, 0:1] = jnp.where(inner, top, jnp.where(lane == 0, corner, 0.0))[:, :ROWS]
    spread = spread_ref[0]
    for row in range(GRID):
        start = (GRID - 1 - row) * GRID
        window = pltpu.roll(spread, (1 - start) % WINDOW, 1)[:GRID, :WIDE]
        window = jnp.where(inner, window, jnp.where(lane == 0, left, 0.0))
        bias_ref[0, 1 + row * GRID : 1 + (row + 1) * GRID] = window[:, :ROWS]


def biases_from_tables(tables):
    inner = tables[:, : SIDE * SIDE].reshape(2, SIDE, SIDE, HEADS)[:, ::-1]
    choice = jnp.asarray(column_choice(), jnp.bfloat16)
    spread = jnp.einsum("lrdh,dc->lhrc", inner, choice, preferred_element_type=jnp.float32)
    spread = spread.reshape(2 * HEADS, SIDE, GRID, GRID).transpose(0, 2, 1, 3)
    spread = spread.reshape(2 * HEADS, GRID, SIDE * GRID)
    spread = jnp.pad(spread, ((0, 0), (0, 16 - GRID), (0, WINDOW - SIDE * GRID)))
    ends = tables[:, SIDE * SIDE :].astype(jnp.float32).transpose(0, 2, 1).reshape(2 * HEADS, 3, 1)
    ends = jnp.broadcast_to(jnp.pad(ends, ((0, 0), (0, 5), (0, 0))), (2 * HEADS, 8, LANES))
    return pl.pallas_call(
        bias_kernel,
        grid=(2 * HEADS,),
        in_specs=[
            pl.BlockSpec((1, 16, WINDOW), lambda i: (i, 0, 0)),
            pl.BlockSpec((1, 8, LANES), lambda i: (i, 0, 0)),
        ],
        out_specs=pl.BlockSpec((1, ROWS, ROWS), lambda i: (i, 0, 0)),
        out_shape=jax.ShapeDtypeStruct((2 * HEADS, ROWS, ROWS), jnp.float32),
        name="bias",
    )(spread, ends)


def table_kernel(grad_ref, spread_ref, ends_ref):
    lane = lax.broadcasted_iota(jnp.int32, (1, ROWS), 1)
    inner = (lane >= 1) & (lane < SEQ)
    total = jnp.zeros((GRID, WINDOW), jnp.float32)
    left = jnp.zeros((1, 1), jnp.float32)
    for row in range(GRID):
        start = (GRID - 1 - row) * GRID
        block = grad_ref[0, 1 + row * GRID : 1 + (row + 1) * GRID]
        left = left + jnp.sum(jnp.where(lane == 0, block, 0.0), keepdims=True)
        block = jnp.where(inner, block, 0.0)
        block = jnp.concatenate([block, jnp.zeros((GRID, WINDOW - ROWS), jnp.float32)], axis=1)
        total = total + pltpu.roll(block, (start - 1) % WINDOW, 1)
    spread_ref[0, :GRID] = total
    spread_ref[0, GRID:] = jnp.zeros((16 - GRID, WINDOW), jnp.float32)
    first = grad_ref[0, 0:1]
    top = jnp.sum(jnp.where(inner, first, 0.0), keepdims=True)
    corner = jnp.sum(jnp.where(lane == 0, first, 0.0), keepdims=True)
    row = lax.broadcasted_iota(jnp.int32, (8, LANES), 0)
    ends_ref[0] = jnp.where(row == 0, top, jnp.where(row == 1, left, corner))


def tables_from_biases(grads):
    pieces = []
    for grad in grads:
        pieces.append(
            pl.pallas_call(
                table_kernel,
                grid=(HEADS,),
                in_specs=[pl.BlockSpec((1, ROWS, ROWS), lambda i: (i, 0, 0))],
                out_specs=[
                    pl.BlockSpec((1, 16, WINDOW), lambda i: (i, 0, 0)),
                    pl.BlockSpec((1, 8, LANES), lambda i: (i, 0, 0)),
                ],
                out_shape=[
                    jax.ShapeDtypeStruct((HEADS, 16, WINDOW), jnp.float32),
                    jax.ShapeDtypeStruct((HEADS, 8, LANES), jnp.float32),
                ],
                name="table_back",
            )(grad)
        )
    spread = jnp.stack([piece[0] for piece in pieces])[:, :, :GRID, : SIDE * GRID]
    ends = jnp.stack([piece[1] for piece in pieces])[:, :, :3, 0].transpose(0, 2, 1)
    spread = spread.reshape(2 * HEADS, GRID, SIDE, GRID).transpose(2, 0, 1, 3)
    spread = spread.reshape(SIDE * 2 * HEADS, PATCHES)
    choice = jnp.asarray(column_choice().T, jnp.bfloat16)
    high = spread.astype(jnp.bfloat16)
    low = (spread - high.astype(jnp.float32)).astype(jnp.bfloat16)
    table = jnp.dot(high, choice, preferred_element_type=jnp.float32) + jnp.dot(
        low, choice, preferred_element_type=jnp.float32
    )
    table = table.reshape(SIDE, 2, HEADS, SIDE)[::-1].transpose(1, 0, 3, 2).reshape(2, SIDE * SIDE, HEADS)
    return jnp.concatenate([table, ends], axis=1)


NT = (((1,), (1,)), ((), ()))
NN = (((1,), (0,)), ((), ()))
TN = (((0,), (0,)), ((), ()))


def product(left, right, dims):
    return lax.dot_general(left, right, dims, preferred_element_type=jnp.float32)


def own_lanes(head):
    lane = lax.broadcasted_iota(jnp.int32, (1, LANES), 1)
    return lane < HEAD if head == 0 else lane >= HEAD


def head_weights(query, key, bias, count, head):
    chosen = jnp.where(own_lanes(head), query, jnp.zeros_like(query))
    scores = product(chosen, key, NT) + bias
    column = lax.broadcasted_iota(jnp.int32, (1, ROWS), 1)
    scores = jnp.where(column < count, scores, NEGATIVE)
    grown = jnp.exp(scores - jnp.max(scores, axis=1, keepdims=True))
    return grown * (1.0 / jnp.sum(grown, axis=1, keepdims=True))


def attention_kernel(pairs, counts_ref, query_ref, key_ref, value_ref, bias_ref, out_ref):
    count = counts_ref[pl.program_id(1)]
    for pair in range(pairs):
        lanes = slice(pair * LANES, (pair + 1) * LANES)
        query, key, value = query_ref[:, lanes], key_ref[:, lanes], value_ref[:, lanes]
        parts = []
        for head in range(2):
            weights = head_weights(query, key, bias_ref[2 * pair + head], count, head)
            parts.append(product(weights.astype(jnp.bfloat16), value, NN))
        out_ref[:, lanes] = jnp.where(own_lanes(0), parts[0], parts[1]).astype(jnp.bfloat16)


def attention_back_kernel(pairs, counts_ref, query_ref, key_ref, value_ref, grad_ref, bias_ref, out_ref, db_ref):
    image = pl.program_id(1)
    count = counts_ref[image]

    @pl.when(image == 0)
    def _():
        db_ref[...] = jnp.zeros_like(db_ref)

    for pair in range(pairs):
        lanes = slice(pair * LANES, (pair + 1) * LANES)
        query, key, value, grad = query_ref[:, lanes], key_ref[:, lanes], value_ref[:, lanes], grad_ref[:, lanes]
        dq, dk, dv = [], [], []
        for head in range(2):
            weights = head_weights(query, key, bias_ref[2 * pair + head], count, head)
            chosen = jnp.where(own_lanes(head), grad, jnp.zeros_like(grad))
            weighted = weights * product(chosen, value, NT)
            dv.append(product(weights.astype(jnp.bfloat16), grad, TN))
            grad_scores = weighted - weights * jnp.sum(weighted, axis=1, keepdims=True)
            low = grad_scores.astype(jnp.bfloat16)
            dq.append(product(low, key, NN))
            dk.append(product(low, query, TN))
            db_ref[2 * pair + head] += grad_scores
        first = own_lanes(0)
        out_ref[0, :, lanes] = (jnp.where(first, dq[0], dq[1]) * HEAD**-0.5).astype(jnp.bfloat16)
        out_ref[1, :, lanes] = jnp.where(first, dk[0], dk[1]).astype(jnp.bfloat16)
        out_ref[2, :, lanes] = jnp.where(first, dv[0], dv[1]).astype(jnp.bfloat16)


def attention_specs(pairs, layer):
    steps = D // LANES // pairs
    lanes = [
        pl.BlockSpec((ROWS, pairs * LANES), lambda step, image, counts, part=part: (image, part * steps + step))
        for part in range(3)
    ]
    bias = pl.BlockSpec((2 * pairs, ROWS, ROWS), lambda step, image, counts: (layer * steps + step, 0, 0))
    return steps, lanes, bias


def attention(counts, qkv, biases, layer, pairs=6):
    steps, lanes, bias_spec = attention_specs(pairs, layer)
    return pl.pallas_call(
        functools.partial(attention_kernel, pairs),
        grid_spec=pltpu.PrefetchScalarGridSpec(
            num_scalar_prefetch=1,
            grid=(steps, qkv.shape[0] // ROWS),
            in_specs=lanes + [bias_spec],
            out_specs=lanes[0],
        ),
        out_shape=jax.ShapeDtypeStruct((qkv.shape[0], D), jnp.bfloat16),
        compiler_params=pltpu.CompilerParams(vmem_limit_bytes=VMEM_LIMIT),
        name="attention",
    )(counts, qkv, qkv, qkv, biases)


def attention_back(counts, qkv, grad, biases, layer, pairs=3):
    steps, lanes, bias_spec = attention_specs(pairs, layer)
    _, _, out_bias_spec = attention_specs(pairs, 0)
    return pl.pallas_call(
        functools.partial(attention_back_kernel, pairs),
        grid_spec=pltpu.PrefetchScalarGridSpec(
            num_scalar_prefetch=1,
            grid=(steps, qkv.shape[0] // ROWS),
            in_specs=lanes + [lanes[0], bias_spec],
            out_specs=[
                pl.BlockSpec((3, ROWS, pairs * LANES), lambda step, image, counts: (0, image, step)),
                out_bias_spec,
            ],
        ),
        out_shape=[
            jax.ShapeDtypeStruct((3, qkv.shape[0], D), jnp.bfloat16),
            jax.ShapeDtypeStruct((HEADS, ROWS, ROWS), jnp.float32),
        ],
        compiler_params=pltpu.CompilerParams(vmem_limit_bytes=VMEM_LIMIT),
        name="attention_back",
    )(counts, qkv, qkv, qkv, grad, biases)


def tile_starts():
    starts, at = {}, 0
    for name, (depth, width) in WEIGHTS.items():
        starts[name] = at
        at += depth // TILE * (width // LANES)
    return starts


FIRST = tile_starts()
MLP_FIRST = FIRST["proj_weight"]
SPAN = 1024


def load_weight(ref, base, name, row, rows, column, columns):
    first, across = FIRST[name] - base, WEIGHTS[name][1] // LANES
    lines = []
    for i in range(rows):
        at = first + (row + i) * across + column
        lines.append(jnp.concatenate([ref[at + j] for j in range(columns)], axis=1))
    return jnp.concatenate(lines, axis=0)


def gelu_and_slope(values):
    size = jnp.abs(values)
    step = 1.0 / (1.0 + (0.3275911 / math.sqrt(2.0)) * size)
    bell = jnp.exp(-0.5 * values * values)
    series = 1.061405429
    for term in (-1.453152027, 1.421413741, -0.284496736, 0.254829592):
        series = series * step + term
    tail = 0.5 * series * step * bell
    area = jnp.where(values < 0, tail, 1.0 - tail)
    return values * area, area + values * bell * (1.0 / math.sqrt(2.0 * math.pi))


def norm_parts(values):
    centre = values - jnp.mean(values, axis=-1, keepdims=True)
    spread = jnp.mean(centre * centre, axis=-1, keepdims=True)
    inverse = lax.rsqrt(spread + EPSILON)
    return centre * inverse, inverse


def norm_back(grad, normal, inverse, gain):
    scaled = grad * gain
    first = jnp.mean(scaled, axis=-1, keepdims=True)
    second = jnp.mean(scaled * normal, axis=-1, keepdims=True)
    return (scaled - first - normal * second) * inverse


def column_sums(values):
    return jnp.sum(values, axis=0, keepdims=True)


def vector(ref, name):
    return ref[ROW[name] : ROW[name] + 1]


def whole_spec(shape):
    return pl.BlockSpec(shape, lambda *_: (0,) * len(shape))


ANYWHERE = pl.BlockSpec(memory_space=pl.ANY)
PARAMS = pltpu.CompilerParams(vmem_limit_bytes=VMEM_LIMIT)


def low_like(*shape):
    return jax.ShapeDtypeStruct(shape, jnp.bfloat16)


def full_like(*shape):
    return jax.ShapeDtypeStruct(shape, jnp.float32)


def project_kernel(places, slots, at_ref, *refs):
    parts, refs = refs[: len(slots)], refs[len(slots) :]
    hidden_ref, vectors_ref, normed_ref, qkv_ref, tiles_ref, whole_ref, sems, out_sem = refs
    copies = copies_between(places, at_ref, parts, slots, whole_ref, sems, True)
    for copy in copies:
        copy.start()
    normal, _ = norm_parts(hidden_ref[...])
    normed_ref[...] = (normal * vector(vectors_ref, "norm1_gain") + vector(vectors_ref, "norm1_bias")).astype(
        jnp.bfloat16
    )
    for copy in copies:
        copy.wait()
    leaving = pltpu.make_async_copy(whole_ref, tiles_ref, out_sem)
    leaving.start()
    across = D // LANES
    for part in range(3):
        weight = load_weight(whole_ref, 0, "qkv_weight", 0, D // TILE, part * across, across)
        rows = product(normed_ref[...], weight, NN)
        if part == 0:
            rows = (rows + vector(vectors_ref, "query_bias")) * HEAD**-0.5
        if part == 2:
            rows = rows + vector(vectors_ref, "value_bias")
        qkv_ref[:, part * D : (part + 1) * D] = rows.astype(jnp.bfloat16)
    leaving.wait()


def project(places, position, parts, hidden, vectors):
    arrays = [array for array, _ in parts]
    slots = [listed for _, listed in parts]
    rows = hidden.shape[0]
    return pl.pallas_call(
        functools.partial(project_kernel, places, slots),
        grid_spec=pltpu.PrefetchScalarGridSpec(
            num_scalar_prefetch=1,
            grid=(1,),
            in_specs=[ANYWHERE] * len(arrays) + [whole_spec((rows, D)), whole_spec(vectors.shape)],
            out_specs=[whole_spec((rows, D)), whole_spec((rows, 3 * D)), ANYWHERE],
            scratch_shapes=[
                pltpu.VMEM((TILES, TILE, LANES), jnp.bfloat16),
                pltpu.SemaphoreType.DMA((sum(len(listed) for listed in slots),)),
                pltpu.SemaphoreType.DMA(()),
            ],
        ),
        out_shape=[low_like(rows, D), low_like(rows, 3 * D), low_like(TILES, TILE, LANES)],
        compiler_params=PARAMS,
        name="project",
    )(position, *arrays, hidden, vectors)


def mlp_weights(tiles_ref, weight_ref, sems, order):
    copies = []
    for i, name in enumerate(order):
        depth, width = WEIGHTS[name]
        count = depth // TILE * (width // LANES)
        here = weight_ref.at[pl.ds(FIRST[name] - MLP_FIRST, count)]
        copies.append(pltpu.make_async_copy(tiles_ref.at[pl.ds(FIRST[name], count)], here, sems.at[i]))
        copies[-1].start()
    return copies


def span_of(step):
    return pl.ds(pl.multiple_of(step * SPAN, SPAN), SPAN)


def mlp_kernel(
    attended_ref,
    hidden_ref,
    vectors_ref,
    fc1_bias_ref,
    tiles_ref,
    result_ref,
    branch_ref,
    middle_ref,
    normed_ref,
    activ_ref,
    slope_ref,
    mlp_ref,
    total_ref,
    weight_ref,
    sems,
):
    copies = mlp_weights(tiles_ref, weight_ref, sems, ("proj_weight", "fc1_weight", "fc2_weight"))
    copies[0].wait()
    across = D // LANES
    weight = load_weight(weight_ref, MLP_FIRST, "proj_weight", 0, D // TILE, 0, across)
    branch = product(attended_ref[...], weight, NN) + vector(vectors_ref, "proj_bias")
    branch_ref[...] = branch.astype(jnp.bfloat16)
    middle_ref[...] = hidden_ref[...] + vector(vectors_ref, "gamma_attn") * branch
    normal, _ = norm_parts(middle_ref[...])
    normed_ref[...] = (normal * vector(vectors_ref, "norm2_gain") + vector(vectors_ref, "norm2_bias")).astype(
        jnp.bfloat16
    )
    total_ref[...] = jnp.broadcast_to(vector(vectors_ref, "fc2_bias"), total_ref.shape)
    copies[1].wait()
    copies[2].wait()

    def step(i, _):
        span = span_of(i)
        weight = load_weight(weight_ref, MLP_FIRST, "fc1_weight", 0, D // TILE, i * (SPAN // LANES), SPAN // LANES)
        activ, slope = gelu_and_slope(product(normed_ref[...], weight, NN) + fc1_bias_ref[:, span])
        activ = activ.astype(jnp.bfloat16)
        activ_ref[:, span] = activ
        slope_ref[:, span] = slope.astype(jnp.bfloat16)
        weight = load_weight(weight_ref, MLP_FIRST, "fc2_weight", i * (SPAN // TILE), SPAN // TILE, 0, across)
        total_ref[...] += product(activ, weight, NN)
        return 0

    lax.fori_loop(0, FF // SPAN, step, 0)
    mlp_ref[...] = total_ref[...].astype(jnp.bfloat16)
    result_ref[...] = middle_ref[...] + vector(vectors_ref, "gamma_mlp") * total_ref[...]


def mlp_scratch(rows):
    return [
        pltpu.VMEM((rows, D), jnp.float32),
        pltpu.VMEM((TILES - MLP_FIRST, TILE, LANES), jnp.bfloat16),
        pltpu.SemaphoreType.DMA((3,)),
    ]


def mlp(attended, hidden, vectors, fc1_bias, tiles):
    rows = hidden.shape[0]
    outs = [full_like(rows, D), low_like(rows, D), full_like(rows, D), low_like(rows, D)]
    outs += [low_like(rows, FF), low_like(rows, FF), low_like(rows, D)]
    ins = [attended, hidden, vectors, fc1_bias]
    return pl.pallas_call(
        mlp_kernel,
        grid=(1,),
        in_specs=[whole_spec(array.shape) for array in ins] + [ANYWHERE],
        out_specs=[whole_spec(out.shape) for out in outs],
        out_shape=outs,
        scratch_shapes=mlp_scratch(rows),
        compiler_params=PARAMS,
        name="mlp",
    )(*ins, tiles)


def mlp_back_kernel(
    grad_ref,
    branch_ref,
    middle_ref,
    slope_ref,
    mlp_ref,
    vectors_ref,
    tiles_ref,
    grad_middle_ref,
    grad_attended_ref,
    grad_mlp_ref,
    grad_pre_ref,
    grad_branch_ref,
    sums_ref,
    fc1_sums_ref,
    total_ref,
    weight_ref,
    sems,
):
    copies = mlp_weights(tiles_ref, weight_ref, sems, ("fc2_weight", "fc1_weight", "proj_weight"))
    across = D // LANES
    grad = grad_ref[...]
    sums_ref[ROW["gamma_mlp"] - 4 : ROW["gamma_mlp"] - 3] = column_sums(grad * mlp_ref[...].astype(jnp.float32))
    grad_mlp = grad * vector(vectors_ref, "gamma_mlp")
    sums_ref[ROW["fc2_bias"] - 4 : ROW["fc2_bias"] - 3] = column_sums(grad_mlp)
    grad_mlp_ref[...] = grad_mlp.astype(jnp.bfloat16)
    total_ref[...] = jnp.zeros_like(total_ref)
    copies[0].wait()
    copies[1].wait()

    def step(i, _):
        span = span_of(i)
        weight = load_weight(weight_ref, MLP_FIRST, "fc2_weight", i * (SPAN // TILE), SPAN // TILE, 0, across)
        grad_pre = product(grad_mlp_ref[...], weight, NT) * slope_ref[:, span].astype(jnp.float32)
        fc1_sums_ref[:, span] = column_sums(grad_pre)
        grad_pre = grad_pre.astype(jnp.bfloat16)
        grad_pre_ref[:, span] = grad_pre
        weight = load_weight(weight_ref, MLP_FIRST, "fc1_weight", 0, D // TILE, i * (SPAN // LANES), SPAN // LANES)
        total_ref[...] += product(grad_pre, weight, NT)
        return 0

    lax.fori_loop(0, FF // SPAN, step, 0)
    normal, inverse = norm_parts(middle_ref[...])
    grad_normed = total_ref[...]
    sums_ref[ROW["norm2_gain"] - 4 : ROW["norm2_gain"] - 3] = column_sums(grad_normed * normal)
    sums_ref[ROW["norm2_bias"] - 4 : ROW["norm2_bias"] - 3] = column_sums(grad_normed)
    grad_middle = grad_ref[...] + norm_back(grad_normed, normal, inverse, vector(vectors_ref, "norm2_gain"))
    grad_middle_ref[...] = grad_middle
    sums_ref[ROW["gamma_attn"] - 4 : ROW["gamma_attn"] - 3] = column_sums(
        grad_middle * branch_ref[...].astype(jnp.float32)
    )
    grad_branch = grad_middle * vector(vectors_ref, "gamma_attn")
    sums_ref[ROW["proj_bias"] - 4 : ROW["proj_bias"] - 3] = column_sums(grad_branch)
    grad_branch_ref[...] = grad_branch.astype(jnp.bfloat16)
    copies[2].wait()
    weight = load_weight(weight_ref, MLP_FIRST, "proj_weight", 0, D // TILE, 0, across)
    grad_attended_ref[...] = product(grad_branch_ref[...], weight, NT).astype(jnp.bfloat16)


def mlp_back(grad, saved, vectors, tiles):
    rows = grad.shape[0]
    outs = [full_like(rows, D), low_like(rows, D), low_like(rows, D), low_like(rows, FF), low_like(rows, D)]
    outs += [full_like(8, D), full_like(1, FF)]
    ins = [grad, saved["branch"], saved["middle"], saved["slope"], saved["mlp_out"], vectors]
    return pl.pallas_call(
        mlp_back_kernel,
        grid=(1,),
        in_specs=[whole_spec(array.shape) for array in ins] + [ANYWHERE],
        out_specs=[whole_spec(out.shape) for out in outs],
        out_shape=outs,
        scratch_shapes=mlp_scratch(rows),
        compiler_params=PARAMS,
        name="mlp_back",
    )(*ins, tiles)


def weight_back_kernel(places, slots, at_ref, *refs):
    normed_ref, project_ref, attended_ref, branch_ref, normed2_ref, pre_ref, activ_ref, mlp_ref = refs[:8]
    parts, (whole_ref, sems) = refs[8 : 8 + len(slots)], refs[8 + len(slots) :]
    across, count = D // LANES, 256 // TILE

    def put(name, row, column, left, grad):
        block = product(left, grad, TN).astype(jnp.bfloat16)
        wide = WEIGHTS[name][1] // LANES
        for i in range(count):
            for j in range(across):
                at = FIRST[name] + (row + i) * wide + column + j
                whole_ref[at] = block[i * TILE : (i + 1) * TILE, j * LANES : (j + 1) * LANES]

    def columns(i):
        return pl.ds(pl.multiple_of(i * 256, 256), 256)

    def narrow(i, _):
        for part in range(3):
            put("qkv_weight", i * count, part * across, normed_ref[:, columns(i)], project_ref[part])
        put("proj_weight", i * count, 0, attended_ref[:, columns(i)], branch_ref[...])
        for part in range(FF // D):
            grad = pre_ref[:, part * D : (part + 1) * D]
            put("fc1_weight", i * count, part * across, normed2_ref[:, columns(i)], grad)
        return 0

    def wide(i, _):
        put("fc2_weight", i * count, 0, activ_ref[:, columns(i)], mlp_ref[...])
        return 0

    lax.fori_loop(0, D // 256, narrow, 0)
    lax.fori_loop(0, FF // 256, wide, 0)
    copies = copies_between(places, at_ref, parts, slots, whole_ref, sems, False)
    for copy in copies:
        copy.start()
    for copy in copies:
        copy.wait()


def weight_back(places, position, slots, ins):
    count = TILES // sum(len(listed) for listed in slots)
    return pl.pallas_call(
        functools.partial(weight_back_kernel, places, slots),
        grid_spec=pltpu.PrefetchScalarGridSpec(
            num_scalar_prefetch=1,
            grid=(1,),
            in_specs=[whole_spec(array.shape) for array in ins],
            out_specs=[ANYWHERE] * len(slots),
            scratch_shapes=[
                pltpu.VMEM((TILES, TILE, LANES), jnp.bfloat16),
                pltpu.SemaphoreType.DMA((sum(len(listed) for listed in slots),)),
            ],
        ),
        out_shape=[low_like(len(listed) * count, TILE, LANES) for listed in slots],
        compiler_params=PARAMS,
        name="weight_back",
    )(position, *ins)


def input_back_kernel(project_ref, grad_middle_ref, hidden_ref, vectors_ref, tiles_ref, out_ref, sums_ref, total_ref):
    across = D // LANES
    for part in range(3):
        weight = load_weight(tiles_ref, 0, "qkv_weight", 0, D // TILE, part * across, across)
        rows = product(project_ref[part], weight, NT)
        total_ref[...] = rows if part == 0 else total_ref[...] + rows
    normal, inverse = norm_parts(hidden_ref[...])
    grad_normed = total_ref[...]
    sums_ref[0:1] = column_sums(grad_normed * normal)
    sums_ref[1:2] = column_sums(grad_normed)
    sums_ref[2:3] = column_sums(project_ref[0].astype(jnp.float32))
    sums_ref[3:4] = column_sums(project_ref[2].astype(jnp.float32))
    out_ref[...] = grad_middle_ref[...] + norm_back(
        grad_normed, normal, inverse, vector(vectors_ref, "norm1_gain")
    )


def input_back(grad_project, grad_middle, hidden, vectors, tiles):
    rows = hidden.shape[0]
    ins = [grad_project, grad_middle, hidden, vectors]
    return pl.pallas_call(
        input_back_kernel,
        grid=(1,),
        in_specs=[whole_spec(array.shape) for array in ins] + [whole_spec((MLP_FIRST, TILE, LANES))],
        out_specs=[whole_spec((rows, D)), whole_spec((8, D))],
        out_shape=[full_like(rows, D), full_like(8, D)],
        scratch_shapes=[pltpu.VMEM((rows, D), jnp.float32)],
        compiler_params=PARAMS,
        name="input_back",
    )(*ins, tiles)


def pad_rows(images):
    padded = jnp.pad(images, ((0, 0), (0, ROWS - SEQ), (0, 0)))
    return padded.reshape(-1, D).astype(jnp.float32)


def cut_rows(rows):
    return rows.reshape(-1, ROWS, D)[:, :SEQ].astype(jnp.bfloat16)


class Places:
    def __init__(self, dp, fsdp):
        low = 2 if dp % 2 == 0 else 1
        core = 2 if fsdp % 2 == 0 else 1
        self.sizes = {"y": low, "x": dp // low, "z": fsdp // core, "c": core}
        self.count = dp * fsdp
        grid = np.arange(self.count).reshape(tuple(self.sizes.values()))
        self.grid = grid
        self.axis = {name: i for i, name in enumerate(self.sizes)}

    def send(self, block, axis, hop):
        target = np.roll(self.grid, -hop, axis=self.axis[axis])
        perm = [(int(a), int(b)) for a, b in zip(self.grid.reshape(-1), target.reshape(-1))]
        return lax.ppermute(block, AXES, perm)

    def fetch(self, block, axis, hop):
        return self.send(block, axis, -hop)

    def total(self, block):
        for axis in ("c", "z", "x", "y"):
            own = block
            for hop in range(1, self.sizes[axis]):
                block = block + self.fetch(own, axis, hop)
        return block

    def position(self, me):
        return jnp.stack([(me // int(np.prod(self.grid.shape[i + 1 :]))) % n for i, n in enumerate(self.grid.shape)])


def block_at(at_ref, places, offset):
    number = 0
    for i, size in enumerate(places.grid.shape):
        number = number * size + lax.rem(at_ref[i] + offset[i], size)
    return number


def copies_between(places, at_ref, parts, slots, whole_ref, sems, inward):
    copies = []
    for part, listed in zip(parts, slots):
        count = part.shape[0] // len(listed)
        for i, slot in enumerate(listed):
            start = 0 if slot is None else block_at(at_ref, places, slot[0]) * (TILES // places.count) + slot[1]
            here, there = part.at[pl.ds(i * count, count)], whole_ref.at[pl.ds(start, count)]
            ends = (here, there) if inward else (there, here)
            copies.append(pltpu.make_async_copy(*ends, sems.at[len(copies)]))
    return copies


def offset_of(**hops):
    return tuple(hops.get(axis, 0) for axis in ("y", "x", "z", "c"))


def tie(*trees):
    leaves, structure = jax.tree.flatten(trees)
    tied = iter(lax.optimization_barrier([leaf for leaf in leaves if isinstance(leaf, jax.Array)]))
    return structure.unflatten([next(tied) if isinstance(leaf, jax.Array) else leaf for leaf in leaves])


def join(blocks):
    return jnp.concatenate(blocks, axis=0) if len(blocks) > 1 else blocks[0]


ORDERS = (("x", "y"), ("y", "x"))


def group_of(shares, offsets):
    half = shares[0].shape[0] // 2
    return [(join([share[part * half : (part + 1) * half] for share in shares]), offsets) for part in range(2)]


def merge(*groups):
    return [(join([group[part][0] for group in groups]), sum((group[part][1] for group in groups), [])) for part in range(2)]


def fetch_column(places, share):
    hops = range(1, places.sizes["z"])
    return [places.fetch(share, "z", hop) for hop in hops], [offset_of(z=hop) for hop in hops]


def fetch_plane(places, group, step):
    arrived = []
    for (block, offsets), order in zip(group, ORDERS):
        at = places.axis[order[step]]
        hops = range(1, places.sizes[order[step]])
        moved = [offset[:at] + (hop,) + offset[at + 1 :] for hop in hops for offset in offsets]
        arrived.append((join([places.fetch(block, order[step], hop) for hop in hops]), moved))
    return arrived


def fetch_core(places, groups):
    half = TILES // places.count // 2
    blocks, slots = [], []
    for group in groups:
        for part, (block, offsets) in enumerate(group):
            blocks.append(block)
            slots.append([(offset, part * half) for offset in offsets])
    whole = join(blocks)
    listed = sum(slots, [])
    parts = [(whole, listed)]
    for hop in range(1, places.sizes["c"]):
        moved = [(offset[:3] + (hop,), first) for offset, first in listed]
        parts.append((places.fetch(whole, "c", hop), moved))
    return parts


def add_low(*blocks):
    total = blocks[0].astype(jnp.float32)
    for block in blocks[1:]:
        total = total + block.astype(jnp.float32)
    return total


def scatter_slots(places):
    half = TILES // places.count // 2
    size = places.sizes
    slots = []
    for part, (first, second) in enumerate(ORDERS):
        for core in range(size["c"]):
            listed = []
            for one in range(size[first]):
                for two in range(size[second]):
                    for z in range(size["z"]):
                        listed.append((offset_of(**{first: one, second: two, "z": z, "c": core}), part * half))
            slots.append(listed)
    return slots


def send_core(places, parts):
    cores = places.sizes["c"]
    halves = [parts[:cores], parts[cores:]]
    return [[mine] + [places.send(other, "c", hop) for hop, other in enumerate(others, 1)] for mine, *others in halves]


def send_plane(places, sums, step):
    result = []
    for blocks, order in zip(sums, ORDERS):
        axis = order[step]
        share = blocks[0].shape[0] // places.sizes[axis]
        cuts = [slice(i * share, (i + 1) * share) for i in range(places.sizes[axis])]
        totals = [add_low(*[block[cut] for block in blocks]).astype(jnp.bfloat16) for cut in cuts]
        result.append([totals[0]] + [places.send(total, axis, hop) for hop, total in enumerate(totals[1:], 1)])
    return result


def send_column(places, sums):
    count = places.sizes["z"]
    share = sums[0][0].shape[0] // count
    totals = []
    for hop in range(count):
        cut = slice(hop * share, (hop + 1) * share)
        totals.append(join([add_low(*[block[cut] for block in blocks]).astype(jnp.bfloat16) for blocks in sums]))
    return [totals[0]] + [places.send(total, "z", hop) for hop, total in enumerate(totals[1:], 1)]


class Layer:
    def __init__(self, number, places, position, counts, vectors, fc1_bias, biases):
        self.number, self.places, self.position, self.counts, self.biases = number, places, position, counts, biases
        self.vectors, self.fc1_bias = vectors[number], fc1_bias[number]

    def forward(self, hidden, parts):
        normed, qkv, self.tiles = project(self.places, self.position, parts, hidden, self.vectors)
        attended = attention(self.counts, qkv, self.biases, self.number)
        result, branch, middle, normed2, activ, slope, mlp_out = mlp(
            attended, hidden, self.vectors, self.fc1_bias, self.tiles
        )
        self.saved = dict(hidden=hidden, normed=normed, qkv=qkv, attended=attended, branch=branch, middle=middle)
        self.saved.update(normed2=normed2, activ=activ, slope=slope, mlp_out=mlp_out)
        return result

    def back_mlp(self, grad):
        return mlp_back(grad, self.saved, self.vectors, self.tiles)

    def back_attention(self, passed):
        return attention_back(self.counts, self.saved["qkv"], passed[1], self.biases, self.number)

    def back_weights(self, passed, grad_project, slots):
        _, _, grad_mlp, grad_pre, grad_branch, _, _ = passed
        saved = self.saved
        ins = [saved["normed"], grad_project, saved["attended"], grad_branch, saved["normed2"], grad_pre]
        return weight_back(self.places, self.position, slots, ins + [saved["activ"], grad_mlp])

    def back_input(self, passed, grad_project):
        return input_back(grad_project, passed[0], self.saved["hidden"], self.vectors, self.tiles)


def scatter_whole(parts):
    whole = parts[0].reshape(-1, LANES)
    return lax.psum_scatter(whole, AXES, scatter_dimension=0, tiled=True).astype(jnp.float32)


def local(dp, fsdp, tokens, counts, params_first, params_second, cotangent):
    devices = dp * fsdp
    places = Places(dp, fsdp)
    stepwise = TILES % (4 * devices) == 0
    tiles = TILES // devices
    me = lax.axis_index(AXES)
    position = places.position(me)
    own, own_smalls = owned_rows(params_first, me, devices)
    if stepwise:
        own = own.reshape(tiles, TILE, LANES)
        column, hops = fetch_column(places, own)
        near = group_of([own], [offset_of()])
        near_first = fetch_plane(places, near, 0)
    params, _ = tie(params_second, own)
    next_own, next_smalls = owned_rows(params, me, devices)
    vectors, fc1_bias, tables = unpack_smalls(places.total(jnp.stack([own_smalls, next_smalls])))
    biases = biases_from_tables(tables)
    first_layer, second_layer = [
        Layer(number, places, position, counts, vectors, fc1_bias, biases) for number in range(2)
    ]
    hidden = pad_rows(tokens)

    if stepwise:
        next_own = next_own.reshape(tiles, TILE, LANES)
        near_second = fetch_plane(places, merge(near, near_first), 1)
        far, next_own = tie(group_of(column, hops), next_own)
        next_column, next_hops = fetch_column(places, next_own)
        far_first = fetch_plane(places, far, 0)
        parts = fetch_core(places, [near, near_first, near_second, far])
        far_second = fetch_plane(places, merge(far, far_first), 1)
        parts += fetch_core(places, [far_first])
        group = group_of([next_own] + next_column, [offset_of()] + next_hops)
        far_second, group = tie(far_second, group)
        parts += fetch_core(places, [far_second])
        first = fetch_plane(places, group, 0)
        next_parts = fetch_core(places, [group])
        first, parts = tie(first, parts)
        second = fetch_plane(places, merge(group, first), 1)
        next_parts += fetch_core(places, [first])
        result = first_layer.forward(hidden, parts)
        second, result = tie(second, result)
        next_parts += fetch_core(places, [second])
    else:
        parts, next_parts = [
            [(lax.all_gather(share, AXES, axis=0, tiled=True).reshape(TILES, TILE, LANES), [None])]
            for share in (own, next_own)
        ]
        result = first_layer.forward(hidden, parts)
    result = second_layer.forward(result, next_parts)
    output = cut_rows(result)

    slots = scatter_slots(places) if stepwise else [[None]]
    next_passed = second_layer.back_mlp(pad_rows(cotangent))
    next_project, next_bias = second_layer.back_attention(next_passed)
    parts = second_layer.back_weights(next_passed, next_project, slots)
    if stepwise:
        sums = send_core(places, parts)
    else:
        next_share = scatter_whole(parts)
    grad, next_sums = second_layer.back_input(next_passed, next_project)
    passed = first_layer.back_mlp(grad)
    if stepwise:
        sums, passed = tie(sums, passed)
        sums = send_plane(places, sums, 0)
    project_grad, bias = first_layer.back_attention(passed)
    parts = first_layer.back_weights(passed, project_grad, slots)
    if stepwise:
        sums, parts = tie(sums, parts)
        sums = send_plane(places, sums, 1)
        own_sums = send_core(places, parts)
        own_sums, sums = tie(own_sums, sums)
        own_sums = send_plane(places, own_sums, 0)
        sums = send_column(places, sums)
        own_sums, sums = tie(own_sums, sums)
        next_share = add_low(*sums).reshape(-1, LANES)
        own_sums = send_column(places, send_plane(places, own_sums, 1))
        share = add_low(*own_sums).reshape(-1, LANES)
    else:
        share = scatter_whole(parts)
    grad, own_row_sums = first_layer.back_input(passed, project_grad)
    vector_grads = jnp.stack(
        [
            jnp.concatenate([row_sums[:4], later[5][: len(VECTORS) - 4]], axis=0)
            for row_sums, later in ((own_row_sums, passed), (next_sums, next_passed))
        ]
    )
    fc1_grads = jnp.stack([passed[6], next_passed[6]])
    table_grads = tables_from_biases([bias, next_bias])
    small_grads = places.total(pack_smalls(vector_grads, fc1_grads, table_grads))
    length = params_first.shape[0] * devices
    grad_first = flat_share(share, small_grads[0], me, devices, length)
    grad_second = flat_share(next_share, small_grads[1], me, devices, length)
    return output, cut_rows(grad), grad_first, grad_second


def solution(mesh):
    return jax.shard_map(
        functools.partial(local, mesh.shape["dp"], mesh.shape["fsdp"]),
        mesh=mesh,
        in_specs=(P(AXES, None, None), P(AXES), P(AXES), P(AXES), P(AXES, None, None)),
        out_specs=(P(AXES, None, None), P(AXES, None, None), P(AXES), P(AXES)),
        check_vma=False,
    )
```

time: 3380 us -> 707 us (0.21)
  local copies, waits for them, and re-layouts: 1130 us -> 71.3 us
  other arithmetic: 1080 us -> 37.6 us
  waiting for transfers between devices: 954 us -> 239 us
  Pallas kernels: 0 us -> 232 us
  matrix products: 153 us -> 20.6 us
  starting transfers between devices: 0.12 us -> 88.9 us
    unnamed x4 -> x0, waiting for transfers between devices: 801 us -> none
    all_gather x2 -> x0, other arithmetic: 602 us -> none  [local(): lax.all_gather(shard_piece, ('dp', 'fsdp'), axis=0, tiled=True)]
    concatenate x4 -> x9, local copies, waits for them, and re-layouts: 488 us -> 8.44 us  [the longest x2 3.39 us: halo(): return jnp.concatenate(pieces, axis=0)]
    scatter-add x2 -> x0, other arithmetic: 415 us -> none  [layer_backward(): jax.ops.segment_sum(grad_table, saved['index_table'].reshape(-1), num_seg...]
    gather x2 -> x0, local copies, waits for them, and re-layouts: 258 us -> none  [layer_forward(): jnp.take(as_float(params, 'relative_table'), index_table.reshape(-1), axi...]
    ppermute x0 -> x62, waiting for transfers between devices: none -> 239 us  [the longest x54 234 us: send(): return lax.ppermute(block, AXES, perm)]
    pallas_call x0 -> x17, Pallas kernels: none -> 232 us  [the longest x2 41.5 us: weight_back(): pl.pallas_call(functools.partial(weight_back_kernel, places, slots), grid...]
    reshape x45 -> x12, local copies, waits for them, and re-layouts: 182 us -> 27.6 us  [the longest x2 9.58 us: biases_from_tables(): spread = spread.reshape(2 * HEADS, GRID, SIDE * GRID)]
  transfers between devices with their start and end apart: 3 -> 62, of which waited for: 2 -> 33; matrix products, arithmetic and copies ran while one was open for 11% -> 14% of each run, Pallas kernels for 0% -> 21%
where the time goes in v1:
time: 707 us; the launch traced here: 693 us
  waiting for transfers between devices  239 us (34%)
  Pallas kernels  232 us (33%)
  starting transfers between devices  88.9 us (13%)
  local copies, waits for them, and re-layouts  71.3 us (10%)
  other arithmetic  37.6 us (5%)
  matrix products  20.6 us (3%)
    ppermute x54, waiting for transfers between devices, send(): return lax.ppermute(block, AXES, perm)  234 us
    ppermute x54, starting transfers between devices, send(): return lax.ppermute(block, AXES, perm)  67.5 us
    pallas_call x2, Pallas kernels, weight_back(): pl.pallas_call(functools.partial(weight_back_kernel, places, slots), grid...  41.5 us
    pallas_call x2, Pallas kernels, mlp(): pl.pallas_call(mlp_kernel, grid=(1,), in_specs=[whole_spec(array.shape) f...  38.7 us
    pallas_call x2, Pallas kernels, attention_back(): pl.pallas_call(functools.partial(attention_back_kernel, pairs), grid_spec...  33.7 us
    pallas_call x2, Pallas kernels, mlp_back(): pl.pallas_call(mlp_back_kernel, grid=(1,), in_specs=[whole_spec(array.sha...  31.1 us
    pallas_call x2, Pallas kernels, project(): pl.pallas_call(functools.partial(project_kernel, places, slots), grid_spe...  28.4 us
    convert_element_type x8, other arithmetic, send_plane(): add_low(*[block[cut] for block in blocks]).astype(jnp.bfloat16)  20.9 us
  transfers between devices with their start and end apart: 62, of which 33 were waited for; matrix products, arithmetic and copies ran while one was open for 14% of the time, Pallas kernels for 21%

profile of v1, /device:TPU:11, one launch (start us, length us, event | category | flops | bytes accessed | tf_op | source)
XLA Modules:
  0.0 692.6 jit_solution(15662508677915534892)
XLA Ops:
  40.6 19.8 %collective-permute-done.3 = bf16[108,16,128]{2,1,0:T(8,128)(2,1)} collective-permute-done((bf16[108,16,128]{2,1,0:T(8,128)(2,1)S(1)}, bf16[108,16,128]{2,1,0:T(8,128)(2,1)}, u32[]{:S(2)}, u32[]{:S(2)}) %collective-permute-start.3) | collective-permute-done | bytes 442400 | tf_op jit(solution)/shard_map/ppermute | solution.py:809
  68.5 10.2 %collective-permute-done.7 = bf16[162,16,128]{2,1,0:T(8,128)(2,1)S(1)} collective-permute-done((bf16[162,16,128]{2,1,0:T(8,128)(2,1)S(1)}, bf16[162,16,128]{2,1,0:T(8,128)(2,1)S(1)}, u32[]{:S(2)}, u32[]{:S(2)}) %collective-permute-start.7) | collective-permute-done | bytes 663584 | tf_op jit(solution)/shard_map/ppermute | solution.py:809
  89.0 7.7 %collective-permute-start.21 = (bf16[756,16,128]{2,1,0:T(8,128)(2,1)S(1)}, bf16[756,16,128]{2,1,0:T(8,128)(2,1)S(1)}, u32[]{:S(2)}, u32[]{:S(2)}) collective-permute-start(bf16[756,16,128]{2,1,0:T(8,128)(2,1)S(1)} %constant_dynamic-update-slice_fusion.2.refs_0_), channel_id=1, source_target_pairs={{0,1},{1,0},{2,3},{3,2},{4,5},{5,4},{6,7},{7,6},{8,9},{9,8},{10,11... | collective-permute-start | bytes 9289736 | tf_op jit(solution)/shard_map/ppermute | solution.py:809
  107.8 9.1 %collective-permute-done.10 = bf16[324,16,128]{2,1,0:T(8,128)(2,1)S(1)} collective-permute-done((bf16[324,16,128]{2,1,0:T(8,128)(2,1)S(1)}, bf16[324,16,128]{2,1,0:T(8,128)(2,1)S(1)}, u32[]{:S(2)}, u32[]{:S(2)}) %collective-permute-start.10) | collective-permute-done | bytes 1327136 | tf_op jit(solution)/shard_map/ppermute | solution.py:809
  136.5 15.2 %collective-permute-done.15 = bf16[216,16,128]{2,1,0:T(8,128)(2,1)S(1)} collective-permute-done((bf16[216,16,128]{2,1,0:T(8,128)(2,1)S(1)}, bf16[216,16,128]{2,1,0:T(8,128)(2,1)S(1)}, u32[]{:S(2)}, u32[]{:S(2)}) %collective-permute-start.15) | collective-permute-done | bytes 884768 | tf_op jit(solution)/shard_map/ppermute | solution.py:809
  161.1 35.0 %collective-permute-done.32 = bf16[2,160,128]{2,1,0:T(8,128)(2,1)S(1)} collective-permute-done((bf16[2,160,128]{2,1,0:T(8,128)(2,1)S(1)}, bf16[2,160,128]{2,1,0:T(8,128)(2,1)S(1)}, u32[]{:S(2)}, u32[]{:S(2)}) %collective-permute-start.32) | collective-permute-done | bytes 81952 | tf_op jit(solution)/shard_map/ppermute | solution.py:809
  214.1 13.9 %bias.1.bias_ref = f32[24,208,208]{2,1,0:T(8,128)} custom-call(f32[24,16,512]{2,1,0:T(8,128)} %pad.34.spread_ref, f32[24,8,128]{2,1,0:T(8,128)} %broadcast_in_dim.28.ends_ref), custom_call_target="tpu_custom_call" | custom-call | tf_op jit(solution)/shard_map/bias/pallas_call | solution.py:233
  229.2 14.1 %project.2 = (bf16[416,768]{1,0:T(8,128)(2,1)}, bf16[416,2304]{1,0:T(8,128)(2,1)}, bf16[3456,16,128]{2,1,0:T(8,128)(2,1)}) custom-call(s32[4]{0:T(128)} %pad_add_fusion.at_ref, bf16[756,16,128]{2,1,0:T(8,128)(2,1)} %copy-done.11, bf16[756,16,128]{2,1,0:T(8,128)(2,1)} %copy-done.23, bf16[324,16,128]{2,1,0:T(8,128)(2,1)} %copy-done.24, ...), custom_call_target="tpu_custom_call" | custom-call | tf_op jit(solution)/shard_map/project/pallas_call | solution.py:514
  250.5 22.8 %mlp.2 = (f32[416,768]{1,0:T(8,128)}, bf16[416,768]{1,0:T(8,128)(2,1)}, f32[416,768]{1,0:T(8,128)}, bf16[416,768]{1,0:T(8,128)(2,1)}, bf16[416,3072]{1,0:T(8,128...) custom-call(bf16[416,768]{1,0:T(8,128)(2,1)} %attention.2.attended_ref.refs_2_, f32[416,768]{1,0:T(8,128)} %bitcast.99, ...), custom_call_target="tpu_custom_call" | custom-call | tf_op jit(solution)/shard_map/mlp/pallas_call | solution.py:609
  295.2 14.3 %project.3 = (bf16[416,768]{1,0:T(8,128)(2,1)}, bf16[416,2304]{1,0:T(8,128)(2,1)}, bf16[3456,16,128]{2,1,0:T(8,128)(2,1)}) custom-call(s32[4]{0:T(128)} %pad_add_fusion.at_ref, bf16[432,16,128]{2,1,0:T(8,128)(2,1)} %copy-done.8, bf16[432,16,128]{2,1,0:T(8,128)(2,1)} %copy-done.25, bf16[432,16,128]{2,1,0:T(8,128)(2,1)} %copy-done.9, ...), custom_call_target="tpu_custom_call" | custom-call | tf_op jit(solution)/shard_map/project/pallas_call | solution.py:514
  316.5 15.8 %mlp.3 = (f32[416,768]{1,0:T(8,128)}, bf16[416,768]{1,0:T(8,128)(2,1)}, f32[416,768]{1,0:T(8,128)}, bf16[416,768]{1,0:T(8,128)(2,1)}, bf16[416,3072]{1,0:T(8,128...) custom-call(bf16[416,768]{1,0:T(8,128)(2,1)} %attention.3.attended_ref.refs_2_, ...), custom_call_target="tpu_custom_call" | custom-call | tf_op jit(solution)/shard_map/mlp/pallas_call | solution.py:609
  332.3 15.3 %mlp_back.2 = (f32[416,768]{1,0:T(8,128)}, bf16[416,768]{1,0:T(8,128)(2,1)}, bf16[416,768]{1,0:T(8,128)(2,1)}, bf16[416,3072]{1,0:T(8,128)(2,1)}, bf16[416,768]{...) custom-call(f32[416,768]{1,0:T(8,128)} %bitcast.102, bf16[416,768]{1,0:T(8,128)(2,1)} %get-tuple-element.138.branch_ref, ...), custom_call_target="tpu_custom_call" | custom-call | tf_op jit(solution)/shard_map/mlp_back/pallas_call | solution.py:685
  347.6 16.9 %attention_back.2 = (bf16[3,416,768]{2,1,0:T(8,128)(2,1)}, f32[12,208,208]{2,1,0:T(8,128)}) custom-call(s32[2]{0:T(128)} %counts_ref.7, bf16[416,2304]{1,0:T(8,128)(2,1)} %get-tuple-element.134.query_ref.key_ref.value_ref, bf16[416,2304]{1,0:T(8,128)(2,1)} %get-tuple-element.134.query_ref.key_ref.value_ref, ...), custom_call_target="tpu_custom_call" | custom-call | tf_op jit(solution)/shard_map/attention_back/pallas_call | solution.py:392
  364.6 20.7 %weight_back.2 = (bf16[864,16,128]{2,1,0:T(8,128)(2,1)}, bf16[864,16,128]{2,1,0:T(8,128)(2,1)}, bf16[864,16,128]{2,1,0:T(8,128)(2,1)}, bf16[864,16,128]{2,1,0:T(8,128)(2,1)}) custom-call(s32[4]{0:T(128)} %pad_add_fusion.at_ref, bf16[416,768]{1,0:T(8,128)(2,1)} %get-tuple-element.137.refs_0_, bf16[3,416,768]{2,1,0:T(8,128)(2,1)} %get-tuple-element.143.refs_1_.project_ref, ...), custom_call_target="tpu_custom_call" | custom-call | tf_op jit(solution)/shard_map/weight_back/pallas_call | solution.py:737
  392.4 15.7 %mlp_back.3 = (f32[416,768]{1,0:T(8,128)}, bf16[416,768]{1,0:T(8,128)(2,1)}, bf16[416,768]{1,0:T(8,128)(2,1)}, bf16[416,3072]{1,0:T(8,128)(2,1)}, bf16[416,768]{...) custom-call(f32[416,768]{1,0:T(8,128)} %get-tuple-element.154.grad_ref, ...), custom_call_target="tpu_custom_call" | custom-call | tf_op jit(solution)/shard_map/mlp_back/pallas_call | solution.py:685
  416.9 16.8 %attention_back.3 = (bf16[3,416,768]{2,1,0:T(8,128)(2,1)}, f32[12,208,208]{2,1,0:T(8,128)}) custom-call(s32[2]{0:T(128)} %counts_ref.7, bf16[416,2304]{1,0:T(8,128)(2,1)} %get-tuple-element.128.query_ref.key_ref.value_ref, bf16[416,2304]{1,0:T(8,128)(2,1)} %get-tuple-element.128.query_ref.key_ref.value_ref, ...), custom_call_target="tpu_custom_call" | custom-call | tf_op jit(solution)/shard_map/attention_back/pallas_call | solution.py:392
  433.6 20.8 %weight_back.3 = (bf16[864,16,128]{2,1,0:T(8,128)(2,1)}, bf16[864,16,128]{2,1,0:T(8,128)(2,1)}, bf16[864,16,128]{2,1,0:T(8,128)(2,1)}, bf16[864,16,128]{2,1,0:T(8,128)(2,1)}) custom-call(s32[4]{0:T(128)} %pad_add_fusion.at_ref, bf16[416,768]{1,0:T(8,128)(2,1)} %get-tuple-element.174.refs_0_, bf16[3,416,768]{2,1,0:T(8,128)(2,1)} %get-tuple-element.167.project_ref.refs_1_, ...), custom_call_target="tpu_custom_call" | custom-call | tf_op jit(solution)/shard_map/weight_back/pallas_call | solution.py:737
  457.1 8.9 %table_back.3 = (f32[12,16,512]{2,1,0:T(8,128)}, f32[12,8,128]{2,1,0:T(8,128)}) custom-call(f32[12,208,208]{2,1,0:T(8,128)} %get-tuple-element.212.grad_ref), custom_call_target="tpu_custom_call" | custom-call | tf_op jit(solution)/shard_map/table_back/pallas_call | solution.py:271
  473.2 8.9 %table_back.2 = (f32[12,16,512]{2,1,0:T(8,128)}, f32[12,8,128]{2,1,0:T(8,128)}) custom-call(f32[12,208,208]{2,1,0:T(8,128)} %get-tuple-element.210.grad_ref), custom_call_target="tpu_custom_call" | custom-call | tf_op jit(solution)/shard_map/table_back/pallas_call | solution.py:271
  558.6 19.7 %collective-permute-done.55 = f32[2,160,128]{2,1,0:T(8,128)S(1)} collective-permute-done((f32[2,160,128]{2,1,0:T(8,128)S(1)}, f32[2,160,128]{2,1,0:T(8,128)S(1)}, u32[]{:S(2)}, u32[]{:S(2)}) %collective-permute-start.55) | collective-permute-done | bytes 163872 | tf_op jit(solution)/shard_map/ppermute | solution.py:809
  584.8 8.6 %collective-permute-done.45 = bf16[108,16,128]{2,1,0:T(8,128)(2,1)S(1)} collective-permute-done((bf16[108,16,128]{2,1,0:T(8,128)(2,1)S(1)}, bf16[108,16,128]{2,1,0:T(8,128)(2,1)S(1)}, u32[]{:S(2)}, u32[]{:S(2)}) %collective-permute-start.45) | collective-permute-done | bytes 442400 | tf_op jit(solution)/shard_map/ppermute | solution.py:809
  604.4 17.8 %collective-permute-done.59 = f32[2,160,128]{2,1,0:T(8,128)S(1)} collective-permute-done((f32[2,160,128]{2,1,0:T(8,128)S(1)}, f32[2,160,128]{2,1,0:T(8,128)S(1)}, u32[]{:S(2)}, u32[]{:S(2)}) %collective-permute-start.59) | collective-permute-done | bytes 163872 | tf_op jit(solution)/shard_map/ppermute | solution.py:809
  637.2 23.1 %collective-permute-done.49 = bf16[108,16,128]{2,1,0:T(8,128)(2,1)S(1)} collective-permute-done((bf16[108,16,128]{2,1,0:T(8,128)(2,1)S(1)}, bf16[108,16,128]{2,1,0:T(8,128)(2,1)S(1)}, u32[]{:S(2)}, u32[]{:S(2)}) %collective-permute-start.49) | collective-permute-done | bytes 442400 | tf_op jit(solution)/shard_map/ppermute | solution.py:809
  660.4 8.5 %collective-permute-done.50 = bf16[108,16,128]{2,1,0:T(8,128)(2,1)S(1)} collective-permute-done((bf16[108,16,128]{2,1,0:T(8,128)(2,1)S(1)}, bf16[108,16,128]{2,1,0:T(8,128)(2,1)S(1)}, u32[]{:S(2)}, u32[]{:S(2)}) %collective-permute-start.50) | collective-permute-done | bytes 442400 | tf_op jit(solution)/shard_map/ppermute | solution.py:809
  (363 shorter events, 310.3 us)
Async XLA Ops:
  24.6 38.8 %collective-permute-start.18 = (bf16[54,16,128]{2,1,0:T(8,128)(2,1)S(1)}, bf16[54,16,128]{2,1,0:T(8,128)(2,1)S(1)}, u32[]{:S(2)}, u32[]{:S(2)}) collective-permute-start(bf16[54,16,128]{2,1,0:T(8,128)(2,1)S(1)} %bitcast.105), channel_id=1, source_target_pairs={{0,16},{1,17},{2,18},{3,19},{4,20},{5,21},{6,22},{7,23},{8,24},{9,... | collective-permute-start | bytes 663560 | tf_op jit(solution)/shard_map/ppermute | solution.py:809
  29.1 31.4 %collective-permute-start.3 = (bf16[108,16,128]{2,1,0:T(8,128)(2,1)S(1)}, bf16[108,16,128]{2,1,0:T(8,128)(2,1)}, u32[]{:S(2)}, u32[]{:S(2)}) collective-permute-start(bf16[108,16,128]{2,1,0:T(8,128)(2,1)S(1)} %bitcast.125), channel_id=1, source_target_pairs={{0,4},{1,5},{2,6},{3,7},{4,0},{5,1},{6,2},{7,3},{8,12},{9,13},{10,... | collective-permute-start | bytes 1327112 | tf_op jit(solution)/shard_map/ppermute | solution.py:809
  65.7 36.6 %collective-permute-start.12 = (bf16[108,16,128]{2,1,0:T(8,128)(2,1)S(1)}, bf16[108,16,128]{2,1,0:T(8,128)(2,1)S(1)}, u32[]{:S(2)}, u32[]{:S(2)}) collective-permute-start(bf16[108,16,128]{2,1,0:T(8,128)(2,1)S(1)} %bitcast.113), channel_id=1, source_target_pairs={{0,4},{1,5},{2,6},{3,7},{4,0},{5,1},{6,2},{7,3},{8,12},{9,13},{10,... | collective-permute-start | bytes 1327112 | tf_op jit(solution)/shard_map/ppermute | solution.py:809
  78.7 28.7 %collective-permute-start.11 = (bf16[108,16,128]{2,1,0:T(8,128)(2,1)S(1)}, bf16[108,16,128]{2,1,0:T(8,128)(2,1)S(1)}, u32[]{:S(2)}, u32[]{:S(2)}) collective-permute-start(bf16[108,16,128]{2,1,0:T(8,128)(2,1)S(1)} %bitcast.114), channel_id=1, source_target_pairs={{0,6},{1,7},{2,0},{3,1},{4,2},{5,3},{6,4},{7,5},{8,14},{9,15},{10,... | collective-permute-start | bytes 1327112 | tf_op jit(solution)/shard_map/ppermute | solution.py:809
  88.2 28.6 %collective-permute-start.10 = (bf16[324,16,128]{2,1,0:T(8,128)(2,1)S(1)}, bf16[324,16,128]{2,1,0:T(8,128)(2,1)S(1)}, u32[]{:S(2)}, u32[]{:S(2)}) collective-permute-start(bf16[324,16,128]{2,1,0:T(8,128)(2,1)S(1)} %pad_maximum_fusion.3), channel_id=1, source_target_pairs={{0,8},{1,9},{2,10},{3,11},{4,12},{5,13},{6,14},{7,15},{8,0},{9,1},... | collective-permute-start | bytes 3981320 | tf_op jit(solution)/shard_map/ppermute | solution.py:809
  89.0 64.4 %collective-permute-start.21 = (bf16[756,16,128]{2,1,0:T(8,128)(2,1)S(1)}, bf16[756,16,128]{2,1,0:T(8,128)(2,1)S(1)}, u32[]{:S(2)}, u32[]{:S(2)}) collective-permute-start(bf16[756,16,128]{2,1,0:T(8,128)(2,1)S(1)} %constant_dynamic-update-slice_fusion.2.refs_0_), channel_id=1, source_target_pairs={{0,1},{1,0},{2,3},{3,2},{4,5},{5,4},{6,7},{7,6},{8,9},{9,8},{10,11... | collective-permute-start | bytes 9289736 | tf_op jit(solution)/shard_map/ppermute | solution.py:809
  117.4 35.9 %collective-permute-start.23 = (bf16[648,16,128]{2,1,0:T(8,128)(2,1)S(1)}, bf16[648,16,128]{2,1,0:T(8,128)(2,1)}, u32[]{:S(2)}, u32[]{:S(2)}) collective-permute-start(bf16[648,16,128]{2,1,0:T(8,128)(2,1)S(1)} %constant_dynamic-update-slice_fusion.12.refs_4_), channel_id=1, source_target_pairs={{0,1},{1,0},{2,3},{3,2},{4,5},{5,4},{6,7},{7,6},{8,9},{9,8},{10,11... | collective-permute-start | bytes 7962632 | tf_op jit(solution)/shard_map/ppermute | solution.py:809
  156.3 117.0 %collective-permute-start.26 = (bf16[432,16,128]{2,1,0:T(8,128)(2,1)}, bf16[432,16,128]{2,1,0:T(8,128)(2,1)}, u32[]{:S(2)}, u32[]{:S(2)}) collective-permute-start(bf16[432,16,128]{2,1,0:T(8,128)(2,1)} %pad_maximum_fusion.1), channel_id=1, source_target_pairs={{0,8},{1,9},{2,10},{3,11},{4,12},{5,13},{6,14},{7,15},{8,0},{9,1},... | collective-permute-start | bytes 5308424 | tf_op jit(solution)/shard_map/ppermute | solution.py:809
  157.1 116.3 %collective-permute-start.25 = (bf16[432,16,128]{2,1,0:T(8,128)(2,1)}, bf16[432,16,128]{2,1,0:T(8,128)(2,1)}, u32[]{:S(2)}, u32[]{:S(2)}) collective-permute-start(bf16[432,16,128]{2,1,0:T(8,128)(2,1)} %pad_maximum_fusion), channel_id=1, source_target_pairs={{0,16},{1,17},{2,18},{3,19},{4,20},{5,21},{6,22},{7,23},{8,24},{9,... | collective-permute-start | bytes 5308424 | tf_op jit(solution)/shard_map/ppermute | solution.py:809
  160.2 35.9 %collective-permute-start.32 = (bf16[2,160,128]{2,1,0:T(8,128)(2,1)S(1)}, bf16[2,160,128]{2,1,0:T(8,128)(2,1)S(1)}, u32[]{:S(2)}, u32[]{:S(2)}) collective-permute-start(bf16[2,160,128]{2,1,0:T(8,128)(2,1)S(1)} %add.250), channel_id=1, source_target_pairs={{0,16},{1,17},{2,18},{3,19},{4,20},{5,21},{6,22},{7,23},{8,24},{9,... | collective-permute-start | bytes 245768 | tf_op jit(solution)/shard_map/ppermute | solution.py:809
  413.0 41.5 %collective-permute-start.36 = (bf16[432,16,128]{2,1,0:T(8,128)(2,1)}, bf16[432,16,128]{2,1,0:T(8,128)(2,1)}, u32[]{:S(2)}, u32[]{:S(2)}) collective-permute-start(bf16[432,16,128]{2,1,0:T(8,128)(2,1)} %get-tuple-element.226), channel_id=1, source_target_pairs={{0,8},{1,9},{2,10},{3,11},{4,12},{5,13},{6,14},{7,15},{8,0},{9,1},... | collective-permute-start | bytes 5308424 | tf_op jit(solution)/shard_map/ppermute | solution.py:809
  416.0 39.6 %collective-permute-start.37 = (bf16[432,16,128]{2,1,0:T(8,128)(2,1)S(1)}, bf16[432,16,128]{2,1,0:T(8,128)(2,1)}, u32[]{:S(2)}, u32[]{:S(2)}) collective-permute-start(bf16[432,16,128]{2,1,0:T(8,128)(2,1)S(1)} %get-tuple-element.224), channel_id=1, source_target_pairs={{0,16},{1,17},{2,18},{3,19},{4,20},{5,21},{6,22},{7,23},{8,24},{9,... | collective-permute-start | bytes 5308424 | tf_op jit(solution)/shard_map/ppermute | solution.py:809
  455.6 74.1 %collective-permute-start.38 = (bf16[864,16,128]{2,1,0:T(8,128)(2,1)}, bf16[864,16,128]{2,1,0:T(8,128)(2,1)}, u32[]{:S(2)}, u32[]{:S(2)}) collective-permute-start(bf16[864,16,128]{2,1,0:T(8,128)(2,1)} %get-tuple-element.185), channel_id=1, source_target_pairs={{0,1},{1,0},{2,3},{3,2},{4,5},{5,4},{6,7},{7,6},{8,9},{9,8},{10,11... | collective-permute-start | bytes 10616840 | tf_op jit(solution)/shard_map/ppermute | solution.py:809
  457.1 72.5 %collective-permute-start.39 = (bf16[864,16,128]{2,1,0:T(8,128)(2,1)}, bf16[864,16,128]{2,1,0:T(8,128)(2,1)}, u32[]{:S(2)}, u32[]{:S(2)}) collective-permute-start(bf16[864,16,128]{2,1,0:T(8,128)(2,1)} %get-tuple-element.187), channel_id=1, source_target_pairs={{0,1},{1,0},{2,3},{3,2},{4,5},{5,4},{6,7},{7,6},{8,9},{9,8},{10,11... | collective-permute-start | bytes 10616840 | tf_op jit(solution)/shard_map/ppermute | solution.py:809
  532.8 64.5 %collective-permute-start.42 = (bf16[432,16,128]{2,1,0:T(8,128)(2,1)S(1)}, bf16[432,16,128]{2,1,0:T(8,128)(2,1)S(1)}, u32[]{:S(2)}, u32[]{:S(2)}) collective-permute-start(bf16[432,16,128]{2,1,0:T(8,128)(2,1)S(1)} %get-tuple-element.222), channel_id=1, source_target_pairs={{0,8},{1,9},{2,10},{3,11},{4,12},{5,13},{6,14},{7,15},{8,0},{9,1},... | collective-permute-start | bytes 5308424 | tf_op jit(solution)/shard_map/ppermute | solution.py:809
  536.9 60.4 %collective-permute-start.43 = (bf16[432,16,128]{2,1,0:T(8,128)(2,1)S(1)}, bf16[432,16,128]{2,1,0:T(8,128)(2,1)S(1)}, u32[]{:S(2)}, u32[]{:S(2)}) collective-permute-start(bf16[432,16,128]{2,1,0:T(8,128)(2,1)S(1)} %get-tuple-element.220), channel_id=1, source_target_pairs={{0,16},{1,17},{2,18},{3,19},{4,20},{5,21},{6,22},{7,23},{8,24},{9,... | collective-permute-start | bytes 5308424 | tf_op jit(solution)/shard_map/ppermute | solution.py:809
  544.2 34.1 %collective-permute-start.55 = (f32[2,160,128]{2,1,0:T(8,128)S(1)}, f32[2,160,128]{2,1,0:T(8,128)S(1)}, u32[]{:S(2)}, u32[]{:S(2)}) collective-permute-start(f32[2,160,128]{2,1,0:T(8,128)S(1)} %fusion.45), channel_id=1, source_target_pairs={{0,6},{1,7},{2,0},{3,1},{4,2},{5,3},{6,4},{7,5},{8,14},{9,15},{10,... | collective-permute-start | bytes 491528 | tf_op jit(solution)/shard_map/ppermute | solution.py:809
  548.8 35.2 %collective-permute-start.44 = (bf16[108,16,128]{2,1,0:T(8,128)(2,1)S(1)}, bf16[108,16,128]{2,1,0:T(8,128)(2,1)S(1)}, u32[]{:S(2)}, u32[]{:S(2)}) collective-permute-start(bf16[108,16,128]{2,1,0:T(8,128)(2,1)S(1)} %pad_maximum_fusion.14), channel_id=1, source_target_pairs={{0,2},{1,3},{2,4},{3,5},{4,6},{5,7},{6,0},{7,1},{8,10},{9,11},{10,... | collective-permute-start | bytes 1327112 | tf_op jit(solution)/shard_map/ppermute | solution.py:809
  555.5 37.9 %collective-permute-start.45 = (bf16[108,16,128]{2,1,0:T(8,128)(2,1)S(1)}, bf16[108,16,128]{2,1,0:T(8,128)(2,1)S(1)}, u32[]{:S(2)}, u32[]{:S(2)}) collective-permute-start(bf16[108,16,128]{2,1,0:T(8,128)(2,1)S(1)} %pad_maximum_fusion.15), channel_id=1, source_target_pairs={{0,4},{1,5},{2,6},{3,7},{4,0},{5,1},{6,2},{7,3},{8,12},{9,13},{10,... | collective-permute-start | bytes 1327112 | tf_op jit(solution)/shard_map/ppermute | solution.py:809
  597.8 30.2 %collective-permute-start.47 = (bf16[216,16,128]{2,1,0:T(8,128)(2,1)S(1)}, bf16[216,16,128]{2,1,0:T(8,128)(2,1)S(1)}, u32[]{:S(2)}, u32[]{:S(2)}) collective-permute-start(bf16[216,16,128]{2,1,0:T(8,128)(2,1)S(1)} %get-tuple-element.229), channel_id=1, source_target_pairs={{0,16},{1,17},{2,18},{3,19},{4,20},{5,21},{6,22},{7,23},{8,24},{9,... | collective-permute-start | bytes 2654216 | tf_op jit(solution)/shard_map/ppermute | solution.py:809
  599.6 28.7 %collective-permute-start.48 = (bf16[216,16,128]{2,1,0:T(8,128)(2,1)S(1)}, bf16[216,16,128]{2,1,0:T(8,128)(2,1)S(1)}, u32[]{:S(2)}, u32[]{:S(2)}) collective-permute-start(bf16[216,16,128]{2,1,0:T(8,128)(2,1)S(1)} %get-tuple-element.231), channel_id=1, source_target_pairs={{0,8},{1,9},{2,10},{3,11},{4,12},{5,13},{6,14},{7,15},{8,0},{9,1},... | collective-permute-start | bytes 2654216 | tf_op jit(solution)/shard_map/ppermute | solution.py:809
  628.5 31.8 %collective-permute-start.49 = (bf16[108,16,128]{2,1,0:T(8,128)(2,1)S(1)}, bf16[108,16,128]{2,1,0:T(8,128)(2,1)S(1)}, u32[]{:S(2)}, u32[]{:S(2)}) collective-permute-start(bf16[108,16,128]{2,1,0:T(8,128)(2,1)S(1)} %pad_maximum_fusion.17), channel_id=1, source_target_pairs={{0,2},{1,3},{2,4},{3,5},{4,6},{5,7},{6,0},{7,1},{8,10},{9,11},{10,... | collective-permute-start | bytes 1327112 | tf_op jit(solution)/shard_map/ppermute | solution.py:809
  628.7 40.2 %collective-permute-start.50 = (bf16[108,16,128]{2,1,0:T(8,128)(2,1)S(1)}, bf16[108,16,128]{2,1,0:T(8,128)(2,1)S(1)}, u32[]{:S(2)}, u32[]{:S(2)}) collective-permute-start(bf16[108,16,128]{2,1,0:T(8,128)(2,1)S(1)} %pad_maximum_fusion.18), channel_id=1, source_target_pairs={{0,4},{1,5},{2,6},{3,7},{4,0},{5,1},{6,2},{7,3},{8,12},{9,13},{10,... | collective-permute-start | bytes 1327112 | tf_op jit(solution)/shard_map/ppermute | solution.py:809
  632.5 40.4 %collective-permute-start.51 = (bf16[108,16,128]{2,1,0:T(8,128)(2,1)S(1)}, bf16[108,16,128]{2,1,0:T(8,128)(2,1)S(1)}, u32[]{:S(2)}, u32[]{:S(2)}) collective-permute-start(bf16[108,16,128]{2,1,0:T(8,128)(2,1)S(1)} %pad_maximum_fusion.19), channel_id=1, source_target_pairs={{0,6},{1,7},{2,0},{3,1},{4,2},{5,3},{6,4},{7,5},{8,14},{9,15},{10,... | collective-permute-start | bytes 1327112 | tf_op jit(solution)/shard_map/ppermute | solution.py:809
  (81 other events, 1014.9 us)

commit v2 on v1

v2 whole, which is shorter than its diff:
```python
import functools
import math

import jax
import jax.numpy as jnp
import numpy as np
from jax import lax
from jax.experimental import pallas as pl
from jax.experimental.pallas import tpu as pltpu
from jax.sharding import PartitionSpec as P

D = 768
HEADS = 12
HEAD = D // HEADS
FF = 3072
GRID = 14
SEQ = 197
RELS = 732
ROWS = 208
LANES = 128
TILE = 16
AXES = ("dp", "fsdp")
VMEM_LIMIT = 56 * 2**20

EPSILON = 1e-06
NEGATIVE = -1000000000.0

ENTRIES = [
    ("norm1_gain", (D,)),
    ("norm1_bias", (D,)),
    ("qkv_weight", (D, 3 * D)),
    ("query_bias", (D,)),
    ("value_bias", (D,)),
    ("relative_table", (RELS, HEADS)),
    ("proj_weight", (D, D)),
    ("proj_bias", (D,)),
    ("gamma_attn", (D,)),
    ("norm2_gain", (D,)),
    ("norm2_bias", (D,)),
    ("fc1_weight", (D, FF)),
    ("fc1_bias", (FF,)),
    ("fc2_weight", (FF, D)),
    ("fc2_bias", (D,)),
    ("gamma_mlp", (D,)),
]
WEIGHTS = {name: dims for name, dims in ENTRIES if name.endswith("weight")}
SIZES = dict(ENTRIES)
VECTORS = [
    "norm1_gain",
    "norm1_bias",
    "query_bias",
    "value_bias",
    "proj_bias",
    "gamma_attn",
    "norm2_gain",
    "norm2_bias",
    "fc2_bias",
    "gamma_mlp",
]
ROW = {name: i for i, name in enumerate(VECTORS)}


def count_rows(dims):
    return -(-math.prod(dims) // LANES)


def virtual_starts():
    starts, at = {}, 0
    for name, dims in ENTRIES:
        starts[name] = at
        at += count_rows(dims)
    return starts, at


STARTS, VIRTUAL = virtual_starts()
SHIFT = RELS * HEADS % LANES
TABLE_END = STARTS["proj_weight"]


def tile_order():
    parts = []
    for name, (depth, width) in WEIGHTS.items():
        across = width // LANES
        rows = STARTS[name] + np.arange(depth * across).reshape(depth // TILE, TILE, across)
        parts.append(rows.transpose(0, 2, 1).reshape(-1))
    return np.concatenate(parts)


def small_order():
    groups = [VECTORS, ["fc1_bias"], ["relative_table"]]
    rows = []
    for group in groups:
        for name in group:
            rows += [STARTS[name] + i for i in range(count_rows(SIZES[name]))]
        rows += [-1] * (-len(rows) % 8)
    return np.array(rows)


TILE_ROWS = tile_order()
SMALL_ROWS = small_order()
TILES = len(TILE_ROWS) // TILE


def tie(*trees):
    leaves, structure = jax.tree.flatten(trees)
    tied = iter(lax.optimization_barrier([leaf for leaf in leaves if isinstance(leaf, jax.Array)]))
    return structure.unflatten([next(tied) if isinstance(leaf, jax.Array) else leaf for leaf in leaves])


def halo(block, before, after, devices, join=True):
    rows = block.shape[-2]
    pieces = [block] if join else []
    for hop in range(1, -(-before // rows) + 1):
        take = min(rows, before - (hop - 1) * rows)
        perm = [(i, i + hop) for i in range(devices - hop)]
        pieces.insert(0, lax.ppermute(block[..., rows - take :, :], AXES, perm))
    for hop in range(1, -(-after // rows) + 1):
        take = min(rows, after - (hop - 1) * rows)
        perm = [(i + hop, i) for i in range(devices - hop)]
        pieces.append(lax.ppermute(block[..., :take, :], AXES, perm))
    return jnp.concatenate(pieces, axis=-2)


def pick_rows(index, source):
    chosen = index[:, None] == lax.broadcasted_iota(jnp.int32, (1, source.shape[0]), 1)
    return jnp.dot(chosen.astype(jnp.bfloat16), source.astype(jnp.bfloat16), preferred_element_type=jnp.float32)


def round_up(value, unit):
    return -(-value // unit) * unit


class Owned:
    def __init__(self, flats, me, devices):
        length = flats[0].shape[0] // LANES
        share = len(TILE_ROWS) // devices
        starts = np.arange(devices)[:, None] * length
        wanted = TILE_ROWS.reshape(devices, share) - starts
        before = round_up(max(0, -wanted.min()) + 1, TILE)
        after = round_up(max(0, wanted.max() + 1 - length), TILE)
        smalls = SMALL_ROWS[None] - starts
        smalls = np.where((smalls >= 0) & (smalls < length), smalls + before - 1, -1)
        self.wanted = self.mine(wanted + before - 1, me)
        self.smalls = self.mine(smalls, me)
        around = halo(jnp.stack([flat.reshape(length, LANES) for flat in flats]), before, after, devices)
        shifted = jnp.concatenate([around[:, :-1, SHIFT:], around[:, 1:, :SHIFT]], axis=2)
        at = me * length - before + 1 + lax.broadcasted_iota(jnp.int32, (1, shifted.shape[1], 1), 1)
        self.virtual = jnp.where(at < TABLE_END, around[:, 1:], shifted)

    @staticmethod
    def mine(table, me):
        return lax.dynamic_index_in_dim(jnp.asarray(table.astype(np.int32)), me, 0, keepdims=False)

    def small_rows(self, *after):
        virtual, *_ = tie(self.virtual, *after)
        return jnp.stack([pick_rows(self.smalls, rows).astype(jnp.bfloat16) for rows in virtual])

    def share(self, number, *after):
        rows = self.virtual[number]
        if after:
            rows, *_ = tie(rows, *after)
        return pick_rows(self.wanted, rows).astype(jnp.bfloat16)


class FlatShare:
    def __init__(self, me, devices, flat_length):
        length = flat_length // LANES // devices
        share = len(TILE_ROWS) // devices
        place = np.full(max(VIRTUAL, devices * length + 1), -1, np.int64)
        place[TILE_ROWS] = np.arange(len(TILE_ROWS))
        small_place = np.full(place.shape, -1, np.int64)
        small_place[SMALL_ROWS[SMALL_ROWS >= 0]] = np.flatnonzero(SMALL_ROWS >= 0)
        span = np.arange(devices)[:, None] * length + np.arange(length + 1)[None]
        relative = place[span] - np.arange(devices)[:, None] * share
        has = place[span] >= 0
        self.before = round_up(max(0, -relative[has].min()), TILE)
        self.after = round_up(max(0, relative[has].max() + 1 - share), TILE)
        smalls_at = self.before + share + self.after
        index = np.where(has, relative + self.before, -1)
        index = np.where(small_place[span] >= 0, small_place[span] + smalls_at, index)
        self.index = Owned.mine(index, me)
        self.at = me * length + lax.broadcasted_iota(jnp.int32, (length, 1), 0)
        self.devices = devices

    def __call__(self, owned, smalls):
        owned = owned.astype(jnp.bfloat16)
        share = owned.shape[0]
        around = halo(owned, self.before, self.after, self.devices, join=False)
        ends = self.before + share
        here = jnp.concatenate([owned, smalls.astype(jnp.bfloat16)], axis=0)
        index = self.index - self.before
        outside = (self.index < self.before) | ((self.index >= ends) & (self.index < ends + self.after))
        index = jnp.where(outside, -1, jnp.where(self.index >= ends, index - self.after, index))
        virtual = pick_rows(index, here)
        index = jnp.where(self.index < self.before, self.index, self.index - share)
        index = jnp.where(outside, index, -1)
        virtual = virtual + pick_rows(index, around)
        here, following = virtual[:-1], virtual[1:]
        lane = lax.broadcasted_iota(jnp.int32, (1, LANES), 1)
        shifted = jnp.concatenate([here[:, LANES - SHIFT :], following[:, : LANES - SHIFT]], axis=1)
        straight = (self.at < TABLE_END - 1) | ((self.at == TABLE_END - 1) & (lane < SHIFT))
        return jnp.where(straight, here, shifted).reshape(-1)


VECTOR_ROWS = D // LANES
FC1_AT = round_up(len(VECTORS) * VECTOR_ROWS, 8)
TABLE_AT = FC1_AT + FF // LANES
TABLE_ROWS = count_rows(SIZES["relative_table"])
LATER = 4


def table_entries(rows):
    table = rows[TABLE_AT : TABLE_AT + TABLE_ROWS].reshape(-1)[: RELS * HEADS].reshape(RELS, HEADS)
    return jnp.pad(table.T, ((0, 16 - HEADS), (0, ENTRY_LANES - RELS)))


def small_gradients(first, later, tables):
    tables = tables.reshape(2, RELS * HEADS)
    tables = jnp.pad(tables, ((0, 0), (0, round_up(TABLE_ROWS, 8) * LANES - RELS * HEADS))).reshape(2, -1, LANES)
    return jnp.concatenate([jnp.stack(first), jnp.stack(later), tables], axis=1)


SIDE = 2 * GRID - 1
WINDOW = round_up(SIDE * GRID, LANES) + LANES
WIDE = round_up(ROWS, LANES)


ENTRY_LANES = round_up(RELS, LANES)
HEAD_ROWS = 2 * 16


def entry_choice(column, transposed):
    shape = (1, WINDOW) if transposed else (WINDOW, 1)
    source = lax.broadcasted_iota(jnp.int32, shape, 1 if transposed else 0)
    group = source // GRID
    target = (SIDE - 1 - group) * SIDE - (source - group * GRID) + GRID - 1 + column
    target = jnp.where(source < SIDE * GRID, target, -1)
    entries = (ENTRY_LANES, 1) if transposed else (1, ENTRY_LANES)
    entry = lax.broadcasted_iota(jnp.int32, entries, 0 if transposed else 1)
    return (entry == target).astype(jnp.float32).astype(jnp.bfloat16)


def bias_kernel(entries_ref, bias_ref, windows_ref):
    for column in range(GRID):
        windows_ref[column] = product(entries_ref[...], entry_choice(column, True), NN)
    lane = lax.broadcasted_iota(jnp.int32, (1, WIDE), 1)
    inner = (lane >= 1) & (lane < SEQ)

    def head(i, _):
        ends = entries_ref[pl.ds(pl.multiple_of(i // 16 * 16, 16), 16), :].astype(jnp.float32)
        picked = lax.broadcasted_iota(jnp.int32, (16, 1), 0) == i % 16
        ends = jnp.sum(jnp.where(picked, ends, 0.0), axis=0, keepdims=True)
        top, left, corner = [ends[:, RELS - k : RELS - k + 1] for k in (3, 2, 1)]
        bias_ref[i] = jnp.zeros(bias_ref.shape[1:], jnp.float32)
        bias_ref[i, 0:1] = jnp.where(inner, top, jnp.where(lane == 0, corner, 0.0))[:, :ROWS]
        spread = jnp.concatenate([windows_ref[column, pl.ds(i, 1)] for column in range(GRID)], axis=0)
        for row in range(GRID):
            start = (GRID - 1 - row) * GRID
            window = pltpu.roll(spread, (1 - start) % WINDOW, 1)[:, :WIDE]
            window = jnp.where(inner, window, jnp.where(lane == 0, left, 0.0))
            bias_ref[i, 1 + row * GRID : 1 + (row + 1) * GRID] = window[:, :ROWS]
        return 0

    lax.fori_loop(0, HEADS, head, 0)


def bias_of(entries):
    return pl.pallas_call(
        bias_kernel,
        grid=(1,),
        in_specs=[pl.BlockSpec(entries.shape, lambda i: (0, 0))],
        out_specs=pl.BlockSpec((HEADS, ROWS, ROWS), lambda i: (0, 0, 0)),
        out_shape=jax.ShapeDtypeStruct((HEADS, ROWS, ROWS), jnp.float32),
        scratch_shapes=[pltpu.VMEM((GRID, 16, WINDOW), jnp.float32)],
        compiler_params=pltpu.CompilerParams(vmem_limit_bytes=VMEM_LIMIT),
        name="bias",
    )(entries)


def table_kernel(first_ref, second_ref, out_ref, windows_ref, ends_ref):
    lane = lax.broadcasted_iota(jnp.int32, (1, ROWS), 1)
    inner = (lane >= 1) & (lane < SEQ)
    entry = lax.broadcasted_iota(jnp.int32, (1, ENTRY_LANES), 1)
    windows_ref[...] = jnp.zeros_like(windows_ref)
    ends_ref[...] = jnp.zeros_like(ends_ref)
    for number, grad_ref in enumerate((first_ref, second_ref)):

        def head(i, _, number=number, grad_ref=grad_ref):
            total = jnp.zeros((GRID, WINDOW), jnp.float32)
            left = jnp.zeros((1, 1), jnp.float32)
            for row in range(GRID):
                start = (GRID - 1 - row) * GRID
                block = grad_ref[i, 1 + row * GRID : 1 + (row + 1) * GRID]
                left = left + jnp.sum(jnp.where(lane == 0, block, 0.0), keepdims=True)
                block = jnp.where(inner, block, 0.0)
                block = jnp.concatenate([block, jnp.zeros((GRID, WINDOW - ROWS), jnp.float32)], axis=1)
                total = total + pltpu.roll(block, (start - 1) % WINDOW, 1)
            at = pl.ds(number * 16 + i, 1)
            for column in range(GRID):
                windows_ref[column, at] = total[column : column + 1]
            first = grad_ref[i, 0:1]
            top = jnp.sum(jnp.where(inner, first, 0.0), keepdims=True)
            corner = jnp.sum(jnp.where(lane == 0, first, 0.0), keepdims=True)
            ends = jnp.where(entry == RELS - 3, top, jnp.where(entry == RELS - 2, left, 0.0))
            ends_ref[at] = jnp.where(entry == RELS - 1, corner, ends)
            return 0

        lax.fori_loop(0, HEADS, head, 0)
    out_ref[...] = ends_ref[...]
    for column in range(GRID):
        rows = windows_ref[column]
        high = rows.astype(jnp.bfloat16)
        low = (rows - high.astype(jnp.float32)).astype(jnp.bfloat16)
        chosen = entry_choice(column, False)
        out_ref[...] += product(high, chosen, NN) + product(low, chosen, NN)


def tables_from_biases(first, second):
    entries = pl.pallas_call(
        table_kernel,
        grid=(1,),
        in_specs=[pl.BlockSpec(first.shape, lambda i: (0, 0, 0))] * 2,
        out_specs=pl.BlockSpec((HEAD_ROWS, ENTRY_LANES), lambda i: (0, 0)),
        out_shape=jax.ShapeDtypeStruct((HEAD_ROWS, ENTRY_LANES), jnp.float32),
        scratch_shapes=[
            pltpu.VMEM((GRID, HEAD_ROWS, WINDOW), jnp.float32),
            pltpu.VMEM((HEAD_ROWS, ENTRY_LANES), jnp.float32),
        ],
        compiler_params=pltpu.CompilerParams(vmem_limit_bytes=VMEM_LIMIT),
        name="table_back",
    )(first, second)
    return entries.reshape(2, 16, ENTRY_LANES)[:, :HEADS, :RELS].transpose(0, 2, 1)


NT = (((1,), (1,)), ((), ()))
NN = (((1,), (0,)), ((), ()))
TN = (((0,), (0,)), ((), ()))


def product(left, right, dims):
    return lax.dot_general(left, right, dims, preferred_element_type=jnp.float32)


def own_lanes(head):
    lane = lax.broadcasted_iota(jnp.int32, (1, LANES), 1)
    return lane < HEAD if head == 0 else lane >= HEAD


def head_weights(query, key, bias, count, head):
    chosen = jnp.where(own_lanes(head), query, jnp.zeros_like(query))
    scores = product(chosen, key, NT) + bias
    column = lax.broadcasted_iota(jnp.int32, (1, ROWS), 1)
    scores = jnp.where(column < count, scores, NEGATIVE)
    grown = jnp.exp(scores - jnp.max(scores, axis=1, keepdims=True))
    return grown * (1.0 / jnp.sum(grown, axis=1, keepdims=True))


def attention_kernel(pairs, counts_ref, query_ref, key_ref, value_ref, bias_ref, out_ref):
    count = counts_ref[pl.program_id(1)]
    for pair in range(pairs):
        lanes = slice(pair * LANES, (pair + 1) * LANES)
        query, key, value = query_ref[:, lanes], key_ref[:, lanes], value_ref[:, lanes]
        parts = []
        for head in range(2):
            weights = head_weights(query, key, bias_ref[2 * pair + head], count, head)
            parts.append(product(weights.astype(jnp.bfloat16), value, NN))
        out_ref[:, lanes] = jnp.where(own_lanes(0), parts[0], parts[1]).astype(jnp.bfloat16)


def attention_back_kernel(pairs, counts_ref, query_ref, key_ref, value_ref, grad_ref, bias_ref, out_ref, db_ref):
    image = pl.program_id(1)
    count = counts_ref[image]

    @pl.when(image == 0)
    def _():
        db_ref[...] = jnp.zeros_like(db_ref)

    for pair in range(pairs):
        lanes = slice(pair * LANES, (pair + 1) * LANES)
        query, key, value, grad = query_ref[:, lanes], key_ref[:, lanes], value_ref[:, lanes], grad_ref[:, lanes]
        dq, dk, dv = [], [], []
        for head in range(2):
            weights = head_weights(query, key, bias_ref[2 * pair + head], count, head)
            chosen = jnp.where(own_lanes(head), grad, jnp.zeros_like(grad))
            weighted = weights * product(chosen, value, NT)
            dv.append(product(weights.astype(jnp.bfloat16), grad, TN))
            grad_scores = weighted - weights * jnp.sum(weighted, axis=1, keepdims=True)
            low = grad_scores.astype(jnp.bfloat16)
            dq.append(product(low, key, NN))
            dk.append(product(low, query, TN))
            db_ref[2 * pair + head] += grad_scores
        first = own_lanes(0)
        out_ref[0, :, lanes] = (jnp.where(first, dq[0], dq[1]) * HEAD**-0.5).astype(jnp.bfloat16)
        out_ref[1, :, lanes] = jnp.where(first, dk[0], dk[1]).astype(jnp.bfloat16)
        out_ref[2, :, lanes] = jnp.where(first, dv[0], dv[1]).astype(jnp.bfloat16)


def attention_specs(pairs):
    steps = D // LANES // pairs
    lanes = [
        pl.BlockSpec((ROWS, pairs * LANES), lambda step, image, counts, part=part: (image, part * steps + step))
        for part in range(3)
    ]
    bias = pl.BlockSpec((2 * pairs, ROWS, ROWS), lambda step, image, counts: (step, 0, 0))
    return steps, lanes, bias


def attention(counts, qkv, bias, pairs=6):
    steps, lanes, bias_spec = attention_specs(pairs)
    return pl.pallas_call(
        functools.partial(attention_kernel, pairs),
        grid_spec=pltpu.PrefetchScalarGridSpec(
            num_scalar_prefetch=1,
            grid=(steps, qkv.shape[0] // ROWS),
            in_specs=lanes + [bias_spec],
            out_specs=lanes[0],
        ),
        out_shape=jax.ShapeDtypeStruct((qkv.shape[0], D), jnp.bfloat16),
        compiler_params=pltpu.CompilerParams(vmem_limit_bytes=VMEM_LIMIT),
        name="attention",
    )(counts, qkv, qkv, qkv, bias)


def attention_back(counts, qkv, grad, bias, pairs=3):
    steps, lanes, bias_spec = attention_specs(pairs)
    return pl.pallas_call(
        functools.partial(attention_back_kernel, pairs),
        grid_spec=pltpu.PrefetchScalarGridSpec(
            num_scalar_prefetch=1,
            grid=(steps, qkv.shape[0] // ROWS),
            in_specs=lanes + [lanes[0], bias_spec],
            out_specs=[
                pl.BlockSpec((3, ROWS, pairs * LANES), lambda step, image, counts: (0, image, step)),
                bias_spec,
            ],
        ),
        out_shape=[
            jax.ShapeDtypeStruct((3, qkv.shape[0], D), jnp.bfloat16),
            jax.ShapeDtypeStruct((HEADS, ROWS, ROWS), jnp.float32),
        ],
        compiler_params=pltpu.CompilerParams(vmem_limit_bytes=VMEM_LIMIT),
        name="attention_back",
    )(counts, qkv, qkv, qkv, grad, bias)


def tile_starts():
    starts, at = {}, 0
    for name, (depth, width) in WEIGHTS.items():
        starts[name] = at
        at += depth // TILE * (width // LANES)
    return starts


FIRST = tile_starts()
MLP_FIRST = FIRST["proj_weight"]
SPAN = 1024


def load_weight(ref, base, name, row, rows, column, columns):
    first, across = FIRST[name] - base, WEIGHTS[name][1] // LANES
    lines = []
    for i in range(rows):
        at = first + (row + i) * across + column
        lines.append(jnp.concatenate([ref[at + j] for j in range(columns)], axis=1))
    return jnp.concatenate(lines, axis=0)


def gelu_and_slope(values):
    size = jnp.abs(values)
    step = 1.0 / (1.0 + (0.3275911 / math.sqrt(2.0)) * size)
    bell = jnp.exp(-0.5 * values * values)
    series = 1.061405429
    for term in (-1.453152027, 1.421413741, -0.284496736, 0.254829592):
        series = series * step + term
    tail = 0.5 * series * step * bell
    area = jnp.where(values < 0, tail, 1.0 - tail)
    return values * area, area + values * bell * (1.0 / math.sqrt(2.0 * math.pi))


def norm_parts(values):
    centre = values - jnp.mean(values, axis=-1, keepdims=True)
    spread = jnp.mean(centre * centre, axis=-1, keepdims=True)
    inverse = lax.rsqrt(spread + EPSILON)
    return centre * inverse, inverse


def norm_back(grad, normal, inverse, gain):
    scaled = grad * gain
    first = jnp.mean(scaled, axis=-1, keepdims=True)
    second = jnp.mean(scaled * normal, axis=-1, keepdims=True)
    return (scaled - first - normal * second) * inverse


def wide_row(ref, first, count):
    return jnp.concatenate([ref[first + i : first + i + 1] for i in range(count)], axis=1)


def vector(ref, name):
    return wide_row(ref, ROW[name] * VECTOR_ROWS, VECTOR_ROWS)


def put_vector(ref, row, values):
    sums = jnp.sum(values, axis=0, keepdims=True)
    for i in range(sums.shape[1] // LANES):
        ref[row + i : row + i + 1] = sums[:, i * LANES : (i + 1) * LANES]


def later_row(name):
    return (ROW[name] - LATER) * VECTOR_ROWS


def whole_spec(shape):
    return pl.BlockSpec(shape, lambda *_: (0,) * len(shape))


ANYWHERE = pl.BlockSpec(memory_space=pl.ANY)
PARAMS = pltpu.CompilerParams(vmem_limit_bytes=VMEM_LIMIT)


def low_like(*shape):
    return jax.ShapeDtypeStruct(shape, jnp.bfloat16)


def full_like(*shape):
    return jax.ShapeDtypeStruct(shape, jnp.float32)


def project_kernel(places, slots, at_ref, *refs):
    parts, refs = refs[: len(slots)], refs[len(slots) :]
    hidden_ref, vectors_ref, normed_ref, qkv_ref, tiles_ref, whole_ref, sems, out_sem = refs
    copies = copies_between(places, at_ref, parts, slots, whole_ref, sems, True)
    for copy in copies:
        copy.start()
    normal, _ = norm_parts(hidden_ref[...])
    normed_ref[...] = (normal * vector(vectors_ref, "norm1_gain") + vector(vectors_ref, "norm1_bias")).astype(
        jnp.bfloat16
    )
    for copy in copies:
        copy.wait()
    leaving = pltpu.make_async_copy(whole_ref, tiles_ref, out_sem)
    leaving.start()
    across = D // LANES
    for part in range(3):
        weight = load_weight(whole_ref, 0, "qkv_weight", 0, D // TILE, part * across, across)
        rows = product(normed_ref[...], weight, NN)
        if part == 0:
            rows = (rows + vector(vectors_ref, "query_bias")) * HEAD**-0.5
        if part == 2:
            rows = rows + vector(vectors_ref, "value_bias")
        qkv_ref[:, part * D : (part + 1) * D] = rows.astype(jnp.bfloat16)
    leaving.wait()


def project(places, position, parts, hidden, vectors):
    arrays = [array for array, _ in parts]
    slots = [listed for _, listed in parts]
    rows = hidden.shape[0]
    return pl.pallas_call(
        functools.partial(project_kernel, places, slots),
        grid_spec=pltpu.PrefetchScalarGridSpec(
            num_scalar_prefetch=1,
            grid=(1,),
            in_specs=[ANYWHERE] * len(arrays) + [whole_spec((rows, D)), whole_spec(vectors.shape)],
            out_specs=[whole_spec((rows, D)), whole_spec((rows, 3 * D)), ANYWHERE],
            scratch_shapes=[
                pltpu.VMEM((TILES, TILE, LANES), jnp.bfloat16),
                pltpu.SemaphoreType.DMA((sum(len(listed) for listed in slots),)),
                pltpu.SemaphoreType.DMA(()),
            ],
        ),
        out_shape=[low_like(rows, D), low_like(rows, 3 * D), low_like(TILES, TILE, LANES)],
        compiler_params=PARAMS,
        name="project",
    )(position, *arrays, hidden, vectors)


def mlp_weights(tiles_ref, weight_ref, sems, order):
    copies = []
    for i, name in enumerate(order):
        depth, width = WEIGHTS[name]
        count = depth // TILE * (width // LANES)
        here = weight_ref.at[pl.ds(FIRST[name] - MLP_FIRST, count)]
        copies.append(pltpu.make_async_copy(tiles_ref.at[pl.ds(FIRST[name], count)], here, sems.at[i]))
        copies[-1].start()
    return copies


def span_of(step):
    return pl.ds(pl.multiple_of(step * SPAN, SPAN), SPAN)


def mlp_kernel(
    attended_ref,
    hidden_ref,
    vectors_ref,
    tiles_ref,
    result_ref,
    branch_ref,
    middle_ref,
    normed_ref,
    activ_ref,
    slope_ref,
    mlp_ref,
    total_ref,
    weight_ref,
    sems,
    fc1_bias_ref,
):
    copies = mlp_weights(tiles_ref, weight_ref, sems, ("proj_weight", "fc1_weight", "fc2_weight"))
    fc1_bias_ref[...] = wide_row(vectors_ref, FC1_AT, FF // LANES)
    copies[0].wait()
    across = D // LANES
    weight = load_weight(weight_ref, MLP_FIRST, "proj_weight", 0, D // TILE, 0, across)
    branch = product(attended_ref[...], weight, NN) + vector(vectors_ref, "proj_bias")
    branch_ref[...] = branch.astype(jnp.bfloat16)
    middle_ref[...] = hidden_ref[...] + vector(vectors_ref, "gamma_attn") * branch
    normal, _ = norm_parts(middle_ref[...])
    normed_ref[...] = (normal * vector(vectors_ref, "norm2_gain") + vector(vectors_ref, "norm2_bias")).astype(
        jnp.bfloat16
    )
    total_ref[...] = jnp.broadcast_to(vector(vectors_ref, "fc2_bias"), total_ref.shape)
    copies[1].wait()
    copies[2].wait()

    def step(i, _):
        span = span_of(i)
        weight = load_weight(weight_ref, MLP_FIRST, "fc1_weight", 0, D // TILE, i * (SPAN // LANES), SPAN // LANES)
        activ, slope = gelu_and_slope(product(normed_ref[...], weight, NN) + fc1_bias_ref[:, span])
        activ = activ.astype(jnp.bfloat16)
        activ_ref[:, span] = activ
        slope_ref[:, span] = slope.astype(jnp.bfloat16)
        weight = load_weight(weight_ref, MLP_FIRST, "fc2_weight", i * (SPAN // TILE), SPAN // TILE, 0, across)
        total_ref[...] += product(activ, weight, NN)
        return 0

    lax.fori_loop(0, FF // SPAN, step, 0)
    mlp_ref[...] = total_ref[...].astype(jnp.bfloat16)
    result_ref[...] = middle_ref[...] + vector(vectors_ref, "gamma_mlp") * total_ref[...]


def mlp_scratch(rows):
    return [
        pltpu.VMEM((rows, D), jnp.float32),
        pltpu.VMEM((TILES - MLP_FIRST, TILE, LANES), jnp.bfloat16),
        pltpu.SemaphoreType.DMA((3,)),
    ]


def mlp(attended, hidden, vectors, tiles):
    rows = hidden.shape[0]
    outs = [full_like(rows, D), low_like(rows, D), full_like(rows, D), low_like(rows, D)]
    outs += [low_like(rows, FF), low_like(rows, FF), low_like(rows, D)]
    ins = [attended, hidden, vectors]
    return pl.pallas_call(
        mlp_kernel,
        grid=(1,),
        in_specs=[whole_spec(array.shape) for array in ins] + [ANYWHERE],
        out_specs=[whole_spec(out.shape) for out in outs],
        out_shape=outs,
        scratch_shapes=mlp_scratch(rows) + [pltpu.VMEM((1, FF), jnp.float32)],
        compiler_params=PARAMS,
        name="mlp",
    )(*ins, tiles)


def mlp_back_kernel(
    grad_ref,
    branch_ref,
    middle_ref,
    slope_ref,
    mlp_ref,
    vectors_ref,
    tiles_ref,
    grad_middle_ref,
    grad_attended_ref,
    grad_mlp_ref,
    grad_pre_ref,
    grad_branch_ref,
    sums_ref,
    total_ref,
    weight_ref,
    sems,
):
    copies = mlp_weights(tiles_ref, weight_ref, sems, ("fc2_weight", "fc1_weight", "proj_weight"))
    across = D // LANES
    grad = grad_ref[...]
    sums_ref[...] = jnp.zeros_like(sums_ref)
    put_vector(sums_ref, later_row("gamma_mlp"), grad * mlp_ref[...].astype(jnp.float32))
    grad_mlp = grad * vector(vectors_ref, "gamma_mlp")
    put_vector(sums_ref, later_row("fc2_bias"), grad_mlp)
    grad_mlp_ref[...] = grad_mlp.astype(jnp.bfloat16)
    total_ref[...] = jnp.zeros_like(total_ref)
    copies[0].wait()
    copies[1].wait()

    def step(i, _):
        span = span_of(i)
        weight = load_weight(weight_ref, MLP_FIRST, "fc2_weight", i * (SPAN // TILE), SPAN // TILE, 0, across)
        grad_pre = product(grad_mlp_ref[...], weight, NT) * slope_ref[:, span].astype(jnp.float32)
        sums = jnp.sum(grad_pre, axis=0, keepdims=True)
        sums = jnp.concatenate([sums[:, k * LANES : (k + 1) * LANES] for k in range(SPAN // LANES)], axis=0)
        first = FC1_AT - LATER * VECTOR_ROWS + i * (SPAN // LANES)
        sums_ref[pl.ds(pl.multiple_of(first, SPAN // LANES), SPAN // LANES)] = sums
        grad_pre = grad_pre.astype(jnp.bfloat16)
        grad_pre_ref[:, span] = grad_pre
        weight = load_weight(weight_ref, MLP_FIRST, "fc1_weight", 0, D // TILE, i * (SPAN // LANES), SPAN // LANES)
        total_ref[...] += product(grad_pre, weight, NT)
        return 0

    lax.fori_loop(0, FF // SPAN, step, 0)
    normal, inverse = norm_parts(middle_ref[...])
    grad_normed = total_ref[...]
    put_vector(sums_ref, later_row("norm2_gain"), grad_normed * normal)
    put_vector(sums_ref, later_row("norm2_bias"), grad_normed)
    grad_middle = grad_ref[...] + norm_back(grad_normed, normal, inverse, vector(vectors_ref, "norm2_gain"))
    grad_middle_ref[...] = grad_middle
    put_vector(sums_ref, later_row("gamma_attn"), grad_middle * branch_ref[...].astype(jnp.float32))
    grad_branch = grad_middle * vector(vectors_ref, "gamma_attn")
    put_vector(sums_ref, later_row("proj_bias"), grad_branch)
    grad_branch_ref[...] = grad_branch.astype(jnp.bfloat16)
    copies[2].wait()
    weight = load_weight(weight_ref, MLP_FIRST, "proj_weight", 0, D // TILE, 0, across)
    grad_attended_ref[...] = product(grad_branch_ref[...], weight, NT).astype(jnp.bfloat16)


def mlp_back(grad, saved, vectors, tiles):
    rows = grad.shape[0]
    outs = [full_like(rows, D), low_like(rows, D), low_like(rows, D), low_like(rows, FF), low_like(rows, D)]
    outs += [full_like(TABLE_AT - LATER * VECTOR_ROWS, LANES)]
    ins = [grad, saved["branch"], saved["middle"], saved["slope"], saved["mlp_out"], vectors]
    return pl.pallas_call(
        mlp_back_kernel,
        grid=(1,),
        in_specs=[whole_spec(array.shape) for array in ins] + [ANYWHERE],
        out_specs=[whole_spec(out.shape) for out in outs],
        out_shape=outs,
        scratch_shapes=mlp_scratch(rows),
        compiler_params=PARAMS,
        name="mlp_back",
    )(*ins, tiles)


def weight_back_kernel(places, slots, at_ref, *refs):
    normed_ref, project_ref, attended_ref, branch_ref, normed2_ref, pre_ref, activ_ref, mlp_ref = refs[:8]
    parts, (whole_ref, sems) = refs[8 : 8 + len(slots)], refs[8 + len(slots) :]
    across, count = D // LANES, 256 // TILE

    def put(name, row, column, left, grad):
        block = product(left, grad, TN).astype(jnp.bfloat16)
        wide = WEIGHTS[name][1] // LANES
        for i in range(count):
            for j in range(across):
                at = FIRST[name] + (row + i) * wide + column + j
                whole_ref[at] = block[i * TILE : (i + 1) * TILE, j * LANES : (j + 1) * LANES]

    def columns(i):
        return pl.ds(pl.multiple_of(i * 256, 256), 256)

    def narrow(i, _):
        for part in range(3):
            put("qkv_weight", i * count, part * across, normed_ref[:, columns(i)], project_ref[part])
        put("proj_weight", i * count, 0, attended_ref[:, columns(i)], branch_ref[...])
        for part in range(FF // D):
            grad = pre_ref[:, part * D : (part + 1) * D]
            put("fc1_weight", i * count, part * across, normed2_ref[:, columns(i)], grad)
        return 0

    def wide(i, _):
        put("fc2_weight", i * count, 0, activ_ref[:, columns(i)], mlp_ref[...])
        return 0

    lax.fori_loop(0, D // 256, narrow, 0)
    lax.fori_loop(0, FF // 256, wide, 0)
    copies = copies_between(places, at_ref, parts, slots, whole_ref, sems, False)
    for copy in copies:
        copy.start()
    for copy in copies:
        copy.wait()


def weight_back(places, position, slots, ins):
    count = TILES // sum(len(listed) for listed in slots)
    return pl.pallas_call(
        functools.partial(weight_back_kernel, places, slots),
        grid_spec=pltpu.PrefetchScalarGridSpec(
            num_scalar_prefetch=1,
            grid=(1,),
            in_specs=[whole_spec(array.shape) for array in ins],
            out_specs=[ANYWHERE] * len(slots),
            scratch_shapes=[
                pltpu.VMEM((TILES, TILE, LANES), jnp.bfloat16),
                pltpu.SemaphoreType.DMA((sum(len(listed) for listed in slots),)),
            ],
        ),
        out_shape=[low_like(len(listed) * count, TILE, LANES) for listed in slots],
        compiler_params=PARAMS,
        name="weight_back",
    )(position, *ins)


def input_back_kernel(project_ref, grad_middle_ref, hidden_ref, vectors_ref, tiles_ref, out_ref, sums_ref, total_ref):
    across = D // LANES
    for part in range(3):
        weight = load_weight(tiles_ref, 0, "qkv_weight", 0, D // TILE, part * across, across)
        rows = product(project_ref[part], weight, NT)
        total_ref[...] = rows if part == 0 else total_ref[...] + rows
    normal, inverse = norm_parts(hidden_ref[...])
    grad_normed = total_ref[...]
    put_vector(sums_ref, 0, grad_normed * normal)
    put_vector(sums_ref, VECTOR_ROWS, grad_normed)
    put_vector(sums_ref, 2 * VECTOR_ROWS, project_ref[0].astype(jnp.float32))
    put_vector(sums_ref, 3 * VECTOR_ROWS, project_ref[2].astype(jnp.float32))
    out_ref[...] = grad_middle_ref[...] + norm_back(
        grad_normed, normal, inverse, vector(vectors_ref, "norm1_gain")
    )


def input_back(grad_project, grad_middle, hidden, vectors, tiles):
    rows = hidden.shape[0]
    ins = [grad_project, grad_middle, hidden, vectors]
    return pl.pallas_call(
        input_back_kernel,
        grid=(1,),
        in_specs=[whole_spec(array.shape) for array in ins] + [whole_spec((MLP_FIRST, TILE, LANES))],
        out_specs=[whole_spec((rows, D)), whole_spec((LATER * VECTOR_ROWS, LANES))],
        out_shape=[full_like(rows, D), full_like(LATER * VECTOR_ROWS, LANES)],
        scratch_shapes=[pltpu.VMEM((rows, D), jnp.float32)],
        compiler_params=PARAMS,
        name="input_back",
    )(*ins, tiles)


def pad_rows(images):
    padded = jnp.pad(images, ((0, 0), (0, ROWS - SEQ), (0, 0)))
    return padded.reshape(-1, D).astype(jnp.float32)


def cut_rows(rows):
    return rows.reshape(-1, ROWS, D)[:, :SEQ].astype(jnp.bfloat16)


class Places:
    def __init__(self, dp, fsdp):
        low = 2 if dp % 2 == 0 else 1
        core = 2 if fsdp % 2 == 0 else 1
        self.sizes = {"y": low, "x": dp // low, "z": fsdp // core, "c": core}
        self.count = dp * fsdp
        grid = np.arange(self.count).reshape(tuple(self.sizes.values()))
        self.grid = grid
        self.axis = {name: i for i, name in enumerate(self.sizes)}

    def exchange(self, block, axis, hop):
        size = self.sizes[axis]
        target = np.take(self.grid, np.arange(size) ^ hop, axis=self.axis[axis])
        perm = [(int(a), int(b)) for a, b in zip(self.grid.reshape(-1), target.reshape(-1))]
        return lax.ppermute(block, AXES, perm)

    def hops(self, axis):
        return range(1, self.sizes[axis])

    def powers(self, axis):
        return [1 << bit for bit in range(self.sizes[axis].bit_length() - 1)]

    def total(self, block, axes):
        for axis in axes:
            for hop in self.powers(axis):
                block = block + self.exchange(block, axis, hop)
        return block

    def position(self, me):
        return jnp.stack([(me // int(np.prod(self.grid.shape[i + 1 :]))) % n for i, n in enumerate(self.grid.shape)])


def block_at(at_ref, places, offset):
    number = 0
    for i, size in enumerate(places.grid.shape):
        number = number * size + (at_ref[i] ^ offset[i])
    return number


def copies_between(places, at_ref, parts, slots, whole_ref, sems, inward):
    copies = []
    for part, listed in zip(parts, slots):
        count = part.shape[0] // len(listed)
        for i, slot in enumerate(listed):
            start = 0 if slot is None else block_at(at_ref, places, slot[0]) * (TILES // places.count) + slot[1]
            here, there = part.at[pl.ds(i * count, count)], whole_ref.at[pl.ds(start, count)]
            ends = (here, there) if inward else (there, here)
            copies.append(pltpu.make_async_copy(*ends, sems.at[len(copies)]))
    return copies


def offset_of(**hops):
    return tuple(hops.get(axis, 0) for axis in ("y", "x", "z", "c"))


def join(blocks):
    return jnp.concatenate(blocks, axis=0) if len(blocks) > 1 else blocks[0]


ORDERS = (("x", "y"), ("y", "x"))


def group_of(shares, offsets):
    half = shares[0].shape[0] // 2
    return [(join([share[part * half : (part + 1) * half] for share in shares]), offsets) for part in range(2)]


def merge(*groups):
    return [(join([group[part][0] for group in groups]), sum((group[part][1] for group in groups), [])) for part in range(2)]


def fetch_column(places, share):
    return [places.exchange(share, "z", hop) for hop in places.hops("z")]


def column_offsets(places):
    return [offset_of(z=hop) for hop in range(places.sizes["z"])]


def fetch_plane(places, group, step):
    arrived = []
    for (block, offsets), order in zip(group, ORDERS):
        at = places.axis[order[step]]
        hops = range(1, places.sizes[order[step]])
        moved = [offset[:at] + (hop,) + offset[at + 1 :] for hop in hops for offset in offsets]
        arrived.append((join([places.exchange(block, order[step], hop) for hop in hops]), moved))
    return arrived


def fetch_plane_with(places, group, step, rows):
    (block, offsets), order = group[0], ORDERS[0]
    count, axis = block.shape[0], order[step]
    hops = range(1, places.sizes[axis])
    arrived = [places.exchange(jnp.concatenate([block, rows], axis=0), axis, hop) for hop in hops]
    moved = [tuple(hop if i == places.axis[axis] else part for i, part in enumerate(o)) for hop in hops for o in offsets]
    rows = sum([piece[count:] for piece in arrived], rows)
    other = fetch_plane(places, group, step)[1]
    return [(join([piece[:count] for piece in arrived]), moved), other], rows


def list_core(places, groups):
    parts = []
    for group in groups:
        half = TILES // places.count // 2
        parts += [(block, [(offset, part * half) for offset in offsets]) for part, (block, offsets) in enumerate(group)]
    return parts


def gather_core(places, groups):
    parts = list_core(places, groups)
    return [(join([block for block, _ in parts]), sum((slots for _, slots in parts), []))]


def fetch_core(places, parts):
    arrived = []
    for hop in range(1, places.sizes["c"]):
        for block, slots in parts:
            moved = [(offset[:3] + (hop,), first) for offset, first in slots]
            arrived.append((places.exchange(block, "c", hop), moved))
    return parts + arrived


def add_low(*blocks):
    total = blocks[0].astype(jnp.float32)
    for block in blocks[1:]:
        total = total + block.astype(jnp.float32)
    return total


def scatter_slots(places):
    half = TILES // places.count // 2
    size = places.sizes
    slots = []
    for part, (first, second) in enumerate(ORDERS):
        for core in range(size["c"]):
            listed = []
            for one in range(size[first]):
                for two in range(size[second]):
                    for z in range(size["z"]):
                        listed.append((offset_of(**{first: one, second: two, "z": z, "c": core}), part * half))
            slots.append(listed)
    return slots


def send_core(places, parts):
    cores = places.sizes["c"]
    halves = [parts[:cores], parts[cores:]]
    return [[mine] + [places.exchange(other, "c", hop) for hop, other in enumerate(others, 1)] for mine, *others in halves]


def plane_totals(places, blocks, axis):
    share = blocks[0].shape[0] // places.sizes[axis]
    cuts = [slice(i * share, (i + 1) * share) for i in range(places.sizes[axis])]
    return [add_low(*[block[cut] for block in blocks]).astype(jnp.bfloat16) for cut in cuts]


def send_totals(places, totals, axis):
    return totals[:1] + [places.exchange(total, axis, hop) for hop, total in enumerate(totals[1:], 1)]


def send_plane(places, sums, step):
    axes = [order[step] for order in ORDERS]
    return [send_totals(places, plane_totals(places, blocks, axis), axis) for blocks, axis in zip(sums, axes)]


def send_plane_tied(places, sums, step, later):
    (first, second), axes = sums, [order[step] for order in ORDERS]
    first, later = tie(first, later)
    first = plane_totals(places, first, axes[0])
    second, first, later = tie(second, first, later)
    result = [send_totals(places, first, axes[0])]
    second, later = tie(plane_totals(places, second, axes[1]), later)
    return result + [send_totals(places, second, axes[1])], later


def column_totals(places, sums):
    count = places.sizes["z"]
    share = sums[0][0].shape[0] // count
    cuts = [slice(hop * share, (hop + 1) * share) for hop in range(count)]
    return [join([add_low(*[block[cut] for block in blocks]).astype(jnp.bfloat16) for blocks in sums]) for cut in cuts]


def send_column(places, totals):
    return [totals[0]] + [places.exchange(total, "z", hop) for hop, total in enumerate(totals[1:], 1)]


class Layer:
    def __init__(self, places, position, counts, vectors):
        self.places, self.position, self.counts, self.vectors = places, position, counts, vectors

    def project(self, hidden, parts):
        normed, qkv, tiles = project(self.places, self.position, parts, hidden, self.vectors)
        self.saved = dict(hidden=hidden, normed=normed, qkv=qkv, tiles=tiles)

    def forward(self):
        saved = self.saved
        saved["attended"] = attention(self.counts, saved["qkv"], self.bias)
        names = ("branch", "middle", "normed2", "activ", "slope", "mlp_out")
        result, *kept = mlp(saved["attended"], saved["hidden"], self.vectors, saved["tiles"])
        saved.update(zip(names, kept))
        return result

    def back_mlp(self, grad):
        return mlp_back(grad, self.saved, self.vectors, self.saved["tiles"])

    def back_attention(self, passed):
        return attention_back(self.counts, self.saved["qkv"], passed[1], self.bias)

    def back_weights(self, passed, grad_project, slots):
        _, _, grad_mlp, grad_pre, grad_branch, _ = passed
        saved = self.saved
        ins = [saved["normed"], grad_project, saved["attended"], grad_branch, saved["normed2"], grad_pre]
        return weight_back(self.places, self.position, slots, ins + [saved["activ"], grad_mlp])

    def back_input(self, passed, grad_project):
        return input_back(grad_project, passed[0], self.saved["hidden"], self.vectors, self.saved["tiles"])


def scatter_whole(parts):
    whole = parts[0].reshape(-1, LANES)
    return lax.psum_scatter(whole, AXES, scatter_dimension=0, tiled=True).astype(jnp.float32)


def local(dp, fsdp, tokens, counts, params_first, params_second, cotangent):
    devices = dp * fsdp
    places = Places(dp, fsdp)
    stepwise = TILES % (4 * devices) == 0 and all(size & (size - 1) == 0 for size in places.sizes.values())
    share_rows = TILES * TILE // devices
    me = lax.axis_index(AXES)
    position = places.position(me)
    owned = Owned([params_first, params_second], me, devices)
    own = owned.share(0)
    small_rows = owned.small_rows(own)
    hidden, grad_output = pad_rows(tokens), pad_rows(cotangent)

    if stepwise:
        own = own.reshape(-1, TILE, LANES)
        column = fetch_column(places, own)
        near, small_rows = tie(group_of([own], [offset_of()]), small_rows)
        small_rows = small_rows.reshape(-1, TILE, LANES)
        near_first, small_rows = fetch_plane_with(places, near, 0, small_rows)
        near_first, small_rows = tie(near_first, small_rows)
        near_second, small_rows = fetch_plane_with(places, merge(near, near_first), 1, small_rows)
        small_rows = places.total(small_rows, "c")
        next_own, near_first = tie(owned.share(1, own), near_first)
        far, near_second = tie(group_of(column, column_offsets(places)[1:]), near_second)
        far_first = fetch_plane(places, far, 0)
        next_own, small_rows, far, hidden, grad_output = tie(next_own, small_rows, far, hidden, grad_output)
        next_own = jnp.concatenate([next_own, small_rows.reshape(-1, LANES)], axis=0)
        next_shares = [next_own] + fetch_column(places, next_own)
        small_rows = sum([rows[share_rows:] for rows in next_shares[1:]], next_own[share_rows:])
        small_rows = small_rows.reshape(2, -1, LANES)
        vectors = small_rows.astype(jnp.float32)
        next_shares = [rows[:share_rows].reshape(-1, TILE, LANES) for rows in next_shares]
        group = group_of(next_shares, column_offsets(places))
        far_second = fetch_plane(places, merge(far, far_first), 1)
        early = gather_core(places, [near, near_first, near_second, far, far_first])
    else:
        small_rows = lax.psum(small_rows, AXES)
    if stepwise:
        far_second, early, group, small_rows, vectors = tie(far_second, early, group, small_rows, vectors)
        parts = fetch_core(places, early) + fetch_core(places, list_core(places, [far_second]))
        first = fetch_plane(places, group, 0)
        first_layer = Layer(places, position, counts, vectors[0])
        first_layer.bias = bias_of(table_entries(small_rows[0]))
        parts, first_layer.bias = tie(parts, first_layer.bias)
        first_layer.project(hidden, parts)
        first, group, first_layer.saved, small_rows = tie(first, group, first_layer.saved, small_rows)
        second = fetch_plane(places, merge(group, first), 1)
        next_parts = fetch_core(places, list_core(places, [first]))
        result = first_layer.forward()
        next_parts, result, small_rows = tie(next_parts, result, small_rows)
        second_bias = bias_of(table_entries(small_rows[1]))
        next_parts += fetch_core(places, gather_core(places, [group]))
        second, next_parts, result, second_bias = tie(second, next_parts, result, second_bias)
        next_parts += fetch_core(places, list_core(places, [second]))
    else:
        vectors = small_rows.astype(jnp.float32)
        second_bias = bias_of(table_entries(small_rows[1]))
        parts, next_parts = [
            [(lax.all_gather(share, AXES, axis=0, tiled=True).reshape(TILES, TILE, LANES), [None])]
            for share in (own, owned.share(1))
        ]
        first_layer = Layer(places, position, counts, vectors[0])
        first_layer.project(hidden, parts)
        first_layer.bias = bias_of(table_entries(small_rows[0]))
        result = first_layer.forward()
    second_layer = Layer(places, position, counts, vectors[1])
    second_layer.bias = second_bias
    second_layer.project(result, next_parts)
    result = second_layer.forward()
    output = cut_rows(result)

    slots = scatter_slots(places) if stepwise else [[None]]
    next_passed = second_layer.back_mlp(grad_output)
    next_project, next_bias = second_layer.back_attention(next_passed)
    parts = second_layer.back_weights(next_passed, next_project, slots)
    if stepwise:
        sums = send_core(places, parts)
    else:
        next_share = scatter_whole(parts)
    grad, next_sums = second_layer.back_input(next_passed, next_project)
    if stepwise:
        sums, grad = send_plane_tied(places, sums, 0, grad)
    passed = first_layer.back_mlp(grad)
    project_grad, bias = first_layer.back_attention(passed)
    if stepwise:
        sums, passed, project_grad = tie(sums, passed, project_grad)
        sums = send_plane(places, sums, 1)
    parts = first_layer.back_weights(passed, project_grad, slots)
    if stepwise:
        sums, parts, passed, project_grad = tie(sums, parts, passed, project_grad)
        own_sums = send_core(places, parts)
        totals = column_totals(places, sums)
        totals, passed, project_grad = tie(totals, passed, project_grad)
    else:
        share = scatter_whole(parts)
    grad, own_row_sums = first_layer.back_input(passed, project_grad)
    if stepwise:
        own_sums, grad, own_row_sums, bias, next_bias = tie(own_sums, grad, own_row_sums, bias, next_bias)
        own_sums, bias = send_plane_tied(places, own_sums, 0, bias)
        totals, bias = tie(totals, bias)
        sums = send_column(places, totals)
    small_grads = small_gradients(
        [own_row_sums, next_sums], [passed[5], next_passed[5]], tables_from_biases(bias, next_bias)
    )
    flat_share = FlatShare(me, devices, params_first.shape[0] * devices)
    if stepwise:
        own_sums, sums, small_grads = tie(own_sums, sums, small_grads)
        own_sums = send_plane(places, own_sums, 1)
        small_grads = places.total(small_grads, "zc")
        own_sums, small_grads = tie(own_sums, small_grads)
        own_sums = send_column(places, column_totals(places, own_sums))
        small_grads = places.total(small_grads, "xy")
        small_grads, sums = tie(small_grads, sums)
        grad_second = flat_share(add_low(*sums).reshape(-1, LANES), small_grads[1])
        own_sums, grad_second, output, grad_tokens = tie(own_sums, grad_second, output, cut_rows(grad))
        share = add_low(*own_sums).reshape(-1, LANES)
    else:
        small_grads = lax.psum(small_grads, AXES)
        grad_second = flat_share(next_share, small_grads[1])
        grad_tokens = cut_rows(grad)
    grad_first = flat_share(share, small_grads[0])
    return output, grad_tokens, grad_first, grad_second


def solution(mesh):
    return jax.shard_map(
        functools.partial(local, mesh.shape["dp"], mesh.shape["fsdp"]),
        mesh=mesh,
        in_specs=(P(AXES, None, None), P(AXES), P(AXES), P(AXES), P(AXES, None, None)),
        out_specs=(P(AXES, None, None), P(AXES, None, None), P(AXES), P(AXES)),
        check_vma=False,
    )
```

time: 707 us -> 535 us (0.76); the launches traced: 693 us -> 530 us
  waiting for transfers between devices: 239 us -> 137 us
  local copies, waits for them, and re-layouts: 71.3 us -> 46.4 us
  starting transfers between devices: 88.9 us -> 66.8 us
  Pallas kernels: 232 us -> 220 us
  matrix products: 20.6 us -> 13.4 us
    ppermute x62 -> x56, waiting for transfers between devices: 239 us -> 137 us  [the longest x50 114 us: exchange(): return lax.ppermute(block, AXES, perm)]
    reshape x12 -> x1, local copies, waits for them, and re-layouts: 27.6 us -> 2.26 us  [small_gradients(): tables = tables.reshape(2, RELS * HEADS)]
    ppermute x62 -> x56, starting transfers between devices: 88.9 us -> 66.8 us  [the longest x50 45.4 us: exchange(): return lax.ppermute(block, AXES, perm)]
    unnamed x104 -> x69, local copies, waits for them, and re-layouts: 10.9 us -> 21.8 us
    transpose x6 -> x0, local copies, waits for them, and re-layouts: 9.51 us -> none  [the longest x1 6.55 us: tables_from_biases(): spread = spread.reshape(2 * HEADS, GRID, SIDE, GRID).transpose(2, 0, 1, 3)]
    dot_general x9 -> x8, matrix products: 20.6 us -> 13.4 us  [pick_rows(): jnp.dot(chosen.astype(jnp.bfloat16), source.astype(jnp.bfloat16), preferr...]
    convert_element_type x13 -> x15, other arithmetic: 24.4 us -> 23.9 us  [the longest x8 20.6 us: plane_totals(): add_low(*[block[cut] for block in blocks]).astype(jnp.bfloat16)]
  transfers between devices with their start and end apart: 62 -> 56, of which waited for: 33 -> 22; matrix products, arithmetic and copies ran while one was open for 14% -> 13% of each run, Pallas kernels for 21% -> 24%
where the time goes in v2:
time: 535 us; the launch traced here: 530 us
  Pallas kernels  220 us (41%)
  waiting for transfers between devices  137 us (26%)
  starting transfers between devices  66.8 us (12%)
  local copies, waits for them, and re-layouts  46.4 us (9%)
  other arithmetic  44.3 us (8%)
  matrix products  13.4 us (3%)
    ppermute x50, waiting for transfers between devices, exchange(): return lax.ppermute(block, AXES, perm)  114 us
    ppermute x50, starting transfers between devices, exchange(): return lax.ppermute(block, AXES, perm)  45.4 us
    pallas_call x2, Pallas kernels, weight_back(): pl.pallas_call(functools.partial(weight_back_kernel, places, slots), grid...  41.8 us
    pallas_call x2, Pallas kernels, attention_back(): pl.pallas_call(functools.partial(attention_back_kernel, pairs), grid_spec...  33.8 us
    pallas_call x2, Pallas kernels, mlp(): pl.pallas_call(mlp_kernel, grid=(1,), in_specs=[whole_spec(array.shape) f...  31.7 us
    pallas_call x2, Pallas kernels, mlp_back(): pl.pallas_call(mlp_back_kernel, grid=(1,), in_specs=[whole_spec(array.sha...  30.3 us
    pallas_call x2, Pallas kernels, project(): pl.pallas_call(functools.partial(project_kernel, places, slots), grid_spe...  28.5 us
    ppermute x3, waiting for transfers between devices, halo(): pieces.append(lax.ppermute(block[..., :take, :], AXES, perm))  22.8 us
  transfers between devices with their start and end apart: 56, of which 22 were waited for; matrix products, arithmetic and copies ran while one was open for 13% of the time, Pallas kernels for 24%

profile of v2, /device:TPU:11, one launch (start us, length us, event | category | flops | bytes accessed | tf_op | source)
XLA Modules:
  0.0 530.2 jit_solution(13646003534373715263)
XLA Ops:
  40.9 18.1 %collective-permute-done.7 = bf16[108,16,128]{2,1,0:T(8,128)(2,1)S(1)} collective-permute-done((bf16[108,16,128]{2,1,0:T(8,128)(2,1)S(1)}, bf16[108,16,128]{2,1,0:T(8,128)(2,1)S(1)}, u32[]{:S(2)}, u32[]{:S(2)}) %collective-permute-start.7) | collective-permute-done | bytes 442400 | tf_op jit(solution)/shard_map/ppermute | solution.py:856
  59.0 8.4 %collective-permute-done.8 = bf16[108,16,128]{2,1,0:T(8,128)(2,1)S(1)} collective-permute-done((bf16[108,16,128]{2,1,0:T(8,128)(2,1)S(1)}, bf16[108,16,128]{2,1,0:T(8,128)(2,1)S(1)}, u32[]{:S(2)}, u32[]{:S(2)}) %collective-permute-start.8) | collective-permute-done | bytes 442400 | tf_op jit(solution)/shard_map/ppermute | solution.py:856
  77.2 8.7 %collective-permute-done.12 = bf16[162,16,128]{2,1,0:T(8,128)(2,1)S(1)} collective-permute-done((bf16[162,16,128]{2,1,0:T(8,128)(2,1)S(1)}, bf16[162,16,128]{2,1,0:T(8,128)(2,1)S(1)}, u32[]{:S(2)}, u32[]{:S(2)}) %collective-permute-start.12) | collective-permute-done | bytes 663584 | tf_op jit(solution)/shard_map/ppermute | solution.py:856
  87.8 6.2 %collective-permute-done.14 = bf16[2048,128]{1,0:T(8,128)(2,1)S(1)} collective-permute-done((bf16[2048,128]{1,0:T(8,128)(2,1)S(1)}, bf16[2048,128]{1,0:T(8,128)(2,1)S(1)}, u32[]{:S(2)}, u32[]{:S(2)}) %collective-permute-start.14) | collective-permute-done | bytes 524320 | tf_op jit(solution)/shard_map/ppermute | solution.py:856
  97.4 22.7 %collective-permute-done.16 = bf16[2048,128]{1,0:T(8,128)(2,1)S(1)} collective-permute-done((bf16[2048,128]{1,0:T(8,128)(2,1)S(1)}, bf16[2048,128]{1,0:T(8,128)(2,1)S(1)}, u32[]{:S(2)}, u32[]{:S(2)}) %collective-permute-start.16) | collective-permute-done | bytes 524320 | tf_op jit(solution)/shard_map/ppermute | solution.py:856
  139.2 14.3 %project.2 = (bf16[416,768]{1,0:T(8,128)(2,1)}, bf16[416,2304]{1,0:T(8,128)(2,1)}, bf16[3456,16,128]{2,1,0:T(8,128)(2,1)}) custom-call(s32[4]{0:T(128)} %pad_add_fusion.at_ref, bf16[1080,16,128]{2,1,0:T(8,128)(2,1)} %constant_dynamic-update-slice_fusion.refs_0_, bf16[1080,16,128]{2,1,0:T(8,128)(2,1)} %collective-permute-done.19.refs_1_, ...), custom_call_target="tpu_custom_call" | custom-call | tf_op jit(solution)/shard_map/project/pallas_call | solution.py:558
  162.7 7.1 %attention.2.attended_ref.refs_2_ = bf16[416,768]{1,0:T(8,128)(2,1)} custom-call(s32[2]{0:T(128)} %counts_ref.7, bf16[416,2304]{1,0:T(8,128)(2,1)} %get-tuple-element.241.query_ref.key_ref.value_ref, bf16[416,2304]{1,0:T(8,128)(2,1)} %get-tuple-element.241.query_ref.key_ref.value_ref, bf16[416,2304]{1,0:T(8,128)(2,1)} %get-tuple-element.241.query_ref.key_ref.value_ref, ...), custom_call_target="tpu_custom_call" | custom-call | tf_op jit(solution)/shard_map/attention/pallas_call | solution.py:410
  169.8 15.9 %mlp.2 = (f32[416,768]{1,0:T(8,128)}, bf16[416,768]{1,0:T(8,128)(2,1)}, f32[416,768]{1,0:T(8,128)}, bf16[416,768]{1,0:T(8,128)(2,1)}, bf16[416,3072]{1,0:T(8,128...) custom-call(bf16[416,768]{1,0:T(8,128)(2,1)} %attention.2.attended_ref.refs_2_, f32[416,768]{1,0:T(8,128)} %bitcast.77, ...), custom_call_target="tpu_custom_call" | custom-call | tf_op jit(solution)/shard_map/mlp/pallas_call | solution.py:654
  208.8 14.2 %project.3 = (bf16[416,768]{1,0:T(8,128)(2,1)}, bf16[416,2304]{1,0:T(8,128)(2,1)}, bf16[3456,16,128]{2,1,0:T(8,128)(2,1)}) custom-call(s32[4]{0:T(128)} %pad_add_fusion.at_ref, bf16[216,16,128]{2,1,0:T(8,128)(2,1)} %copy-done.9, bf16[216,16,128]{2,1,0:T(8,128)(2,1)} %copy-done.11, bf16[216,16,128]{2,1,0:T(8,128)(2,1)} %copy-done.21, ...), custom_call_target="tpu_custom_call" | custom-call | tf_op jit(solution)/shard_map/project/pallas_call | solution.py:558
  223.0 7.5 %attention.3.attended_ref.refs_2_ = bf16[416,768]{1,0:T(8,128)(2,1)} custom-call(s32[2]{0:T(128)} %counts_ref.7, bf16[416,2304]{1,0:T(8,128)(2,1)} %get-tuple-element.263.query_ref.key_ref.value_ref, bf16[416,2304]{1,0:T(8,128)(2,1)} %get-tuple-element.263.query_ref.key_ref.value_ref, bf16[416,2304]{1,0:T(8,128)(2,1)} %get-tuple-element.263.query_ref.key_ref.value_ref, ...), custom_call_target="tpu_custom_call" | custom-call | tf_op jit(solution)/shard_map/attention/pallas_call | solution.py:410
  230.5 15.9 %mlp.3 = (f32[416,768]{1,0:T(8,128)}, bf16[416,768]{1,0:T(8,128)(2,1)}, f32[416,768]{1,0:T(8,128)}, bf16[416,768]{1,0:T(8,128)(2,1)}, bf16[416,3072]{1,0:T(8,128...) custom-call(bf16[416,768]{1,0:T(8,128)(2,1)} %attention.3.attended_ref.refs_2_, ...), custom_call_target="tpu_custom_call" | custom-call | tf_op jit(solution)/shard_map/mlp/pallas_call | solution.py:654
  246.4 15.1 %mlp_back.2 = (f32[416,768]{1,0:T(8,128)}, bf16[416,768]{1,0:T(8,128)(2,1)}, bf16[416,768]{1,0:T(8,128)(2,1)}, bf16[416,3072]{1,0:T(8,128)(2,1)}, bf16[416,768]{1,0:T(8,128)(2,1)}, /*index=5*/f32[64,128]{1,0:T(8,128)}) custom-call(f32[416,768]{1,0:T(8,128)} %bitcast.79, bf16[416,768]{1,0:T(8,128)(2,1)} %get-tuple-element.267.branch_ref, ...), custom_call_target="tpu_custom_call" | custom-call | tf_op jit(solution)/shard_map/mlp_back/pallas_call | solution.py:731
  261.5 16.8 %attention_back.2 = (bf16[3,416,768]{2,1,0:T(8,128)(2,1)}, f32[12,208,208]{2,1,0:T(8,128)}) custom-call(s32[2]{0:T(128)} %counts_ref.7, bf16[416,2304]{1,0:T(8,128)(2,1)} %get-tuple-element.263.query_ref.key_ref.value_ref, bf16[416,2304]{1,0:T(8,128)(2,1)} %get-tuple-element.263.query_ref.key_ref.value_ref, ...), custom_call_target="tpu_custom_call" | custom-call | tf_op jit(solution)/shard_map/attention_back/pallas_call | solution.py:426
  278.3 21.0 %weight_back.2 = (bf16[864,16,128]{2,1,0:T(8,128)(2,1)}, bf16[864,16,128]{2,1,0:T(8,128)(2,1)}, bf16[864,16,128]{2,1,0:T(8,128)(2,1)}, bf16[864,16,128]{2,1,0:T(8,128)(2,1)}) custom-call(s32[4]{0:T(128)} %pad_add_fusion.at_ref, bf16[416,768]{1,0:T(8,128)(2,1)} %get-tuple-element.262.refs_0_, bf16[3,416,768]{2,1,0:T(8,128)(2,1)} %get-tuple-element.272.refs_1_.project_ref, ...), custom_call_target="tpu_custom_call" | custom-call | tf_op jit(solution)/shard_map/weight_back/pallas_call | solution.py:783
  299.8 6.7 %input_back.2 = (f32[416,768]{1,0:T(8,128)}, f32[24,128]{1,0:T(8,128)}) custom-call(bf16[3,416,768]{2,1,0:T(8,128)(2,1)} %get-tuple-element.272.refs_1_.project_ref, f32[416,768]{1,0:T(8,128)} %get-tuple-element.282.grad_middle_ref, f32[416,768]{1,0:T(8,128)} %get-tuple-element.261.refs_10_.hidden_ref, f32[160,128]{1,0:T(8,128)} %get-tuple-element.446.refs_11_.vectors_ref, ...), custom_call_target="tpu_custom_call" | custom-call | tf_op jit(solution)/shard_map/input_back/pallas_call | solution.py:821
  316.6 15.2 %mlp_back.3 = (f32[416,768]{1,0:T(8,128)}, bf16[416,768]{1,0:T(8,128)(2,1)}, bf16[416,768]{1,0:T(8,128)(2,1)}, bf16[416,3072]{1,0:T(8,128)(2,1)}, bf16[416,768]{1,0:T(8,128)(2,1)}, /*index=5*/f32[64,128]{1,0:T(8,128)}) custom-call(f32[416,768]{1,0:T(8,128)} %get-tuple-element.294.grad_ref, bf16[416,768]{1,0:T(8,128)(2,1)} %get-tuple-element.295.branch_ref, ...), custom_call_target="tpu_custom_call" | custom-call | tf_op jit(solution)/shard_map/mlp_back/pallas_call | solution.py:731
  331.8 17.0 %attention_back.3 = (bf16[3,416,768]{2,1,0:T(8,128)(2,1)}, f32[12,208,208]{2,1,0:T(8,128)}) custom-call(s32[2]{0:T(128)} %counts_ref.7, bf16[416,2304]{1,0:T(8,128)(2,1)} %get-tuple-element.241.query_ref.key_ref.value_ref, bf16[416,2304]{1,0:T(8,128)(2,1)} %get-tuple-element.241.query_ref.key_ref.value_ref, ...), custom_call_target="tpu_custom_call" | custom-call | tf_op jit(solution)/shard_map/attention_back/pallas_call | solution.py:426
  348.8 6.3 %collective-permute-done.32 = bf16[432,16,128]{2,1,0:T(8,128)(2,1)S(1)} collective-permute-done((bf16[432,16,128]{2,1,0:T(8,128)(2,1)}, bf16[432,16,128]{2,1,0:T(8,128)(2,1)S(1)}, u32[]{:S(2)}, u32[]{:S(2)}) %collective-permute-start.32) | collective-permute-done | bytes 1769504 | tf_op jit(solution)/shard_map/ppermute | solution.py:856
  358.6 20.8 %weight_back.3 = (bf16[864,16,128]{2,1,0:T(8,128)(2,1)}, bf16[864,16,128]{2,1,0:T(8,128)(2,1)}, bf16[864,16,128]{2,1,0:T(8,128)(2,1)}, bf16[864,16,128]{2,1,0:T(8,128)(2,1)}) custom-call(s32[4]{0:T(128)} %pad_add_fusion.at_ref, bf16[416,768]{1,0:T(8,128)(2,1)} %get-tuple-element.310.refs_0_, bf16[3,416,768]{2,1,0:T(8,128)(2,1)} %get-tuple-element.334.refs_1_.project_ref, ...), custom_call_target="tpu_custom_call" | custom-call | tf_op jit(solution)/shard_map/weight_back/pallas_call | solution.py:783
  386.7 6.7 %input_back.3 = (f32[416,768]{1,0:T(8,128)}, f32[24,128]{1,0:T(8,128)}) custom-call(bf16[3,416,768]{2,1,0:T(8,128)(2,1)} %get-tuple-element.334.refs_1_.project_ref, f32[416,768]{1,0:T(8,128)} %get-tuple-element.335.grad_middle_ref, f32[416,768]{1,0:T(8,128)} %bitcast.78, f32[160,128]{1,0:T(8,128)} %get-tuple-element.447.refs_7_.vectors_ref, ...), custom_call_target="tpu_custom_call" | custom-call | tf_op jit(solution)/shard_map/input_back/pallas_call | solution.py:821
  407.2 15.2 %table_back.1 = f32[32,768]{1,0:T(8,128)} custom-call(f32[12,208,208]{2,1,0:T(8,128)} %get-tuple-element.368.first_ref, f32[12,208,208]{2,1,0:T(8,128)} %get-tuple-element.369.second_ref), custom_call_target="tpu_custom_call" | custom-call | tf_op jit(solution)/shard_map/table_back/pallas_call | solution.py:319
  428.4 17.0 %collective-permute-done.41 = bf16[108,16,128]{2,1,0:T(8,128)(2,1)} collective-permute-done((bf16[108,16,128]{2,1,0:T(8,128)(2,1)}, bf16[108,16,128]{2,1,0:T(8,128)(2,1)}, u32[]{:S(2)}, u32[]{:S(2)}) %collective-permute-start.41) | collective-permute-done | bytes 442400 | tf_op jit(solution)/shard_map/ppermute | solution.py:856
  478.7 8.1 %collective-permute-start.52 = (bf16[384,128]{1,0:T(8,128)(2,1)S(1)}, bf16[384,128]{1,0:T(8,128)(2,1)S(1)}, u32[]{:S(2)}, u32[]{:S(2)}) collective-permute-start(bf16[384,128]{1,0:T(8,128)(2,1)S(1)} %bitcast.118), channel_id=1, source_target_pairs={{0,1},{1,2},{2,3},{3,4},{4,5},{5,6},{6,7},{7,8},{8,9},{9,10},{10,1... | collective-permute-start | bytes 294920 | tf_op jit(solution)/shard_map/ppermute | solution.py:116
  491.4 21.5 %collective-permute-done.53 = bf16[288,128]{1,0:T(8,128)(2,1)S(1)} collective-permute-done((bf16[288,128]{1,0:T(8,128)(2,1)S(1)}, bf16[288,128]{1,0:T(8,128)(2,1)S(1)}, u32[]{:S(2)}, u32[]{:S(2)}) %collective-permute-start.53) | collective-permute-done | bytes 73760 | tf_op jit(solution)/shard_map/ppermute | solution.py:120
  (284 shorter events, 202.2 us)
Async XLA Ops:
  24.3 34.7 %collective-permute-start.7 = (bf16[108,16,128]{2,1,0:T(8,128)(2,1)S(1)}, bf16[108,16,128]{2,1,0:T(8,128)(2,1)S(1)}, u32[]{:S(2)}, u32[]{:S(2)}) collective-permute-start(bf16[108,16,128]{2,1,0:T(8,128)(2,1)S(1)} %bitcast.114), channel_id=1, source_target_pairs={{0,4},{1,5},{2,6},{3,7},{4,0},{5,1},{6,2},{7,3},{8,12},{9,13},{10,... | collective-permute-start | bytes 1327112 | tf_op jit(solution)/shard_map/ppermute | solution.py:856
  30.0 37.4 %collective-permute-start.8 = (bf16[108,16,128]{2,1,0:T(8,128)(2,1)S(1)}, bf16[108,16,128]{2,1,0:T(8,128)(2,1)S(1)}, u32[]{:S(2)}, u32[]{:S(2)}) collective-permute-start(bf16[108,16,128]{2,1,0:T(8,128)(2,1)S(1)} %bitcast.115), channel_id=1, source_target_pairs={{0,6},{1,7},{2,4},{3,5},{4,2},{5,3},{6,0},{7,1},{8,14},{9,15},{10,... | collective-permute-start | bytes 1327112 | tf_op jit(solution)/shard_map/ppermute | solution.py:856
  39.2 28.4 %collective-permute-start.4 = (bf16[128,16,128]{2,1,0:T(8,128)(2,1)S(1)}, bf16[128,16,128]{2,1,0:T(8,128)(2,1)S(1)}, u32[]{:S(2)}, u32[]{:S(2)}) collective-permute-start(bf16[128,16,128]{2,1,0:T(8,128)(2,1)S(1)} %pad_maximum_fusion.9), channel_id=1, source_target_pairs={{0,16},{1,17},{2,18},{3,19},{4,20},{5,21},{6,22},{7,23},{8,24},{9,... | collective-permute-start | bytes 1572872 | tf_op jit(solution)/shard_map/ppermute | solution.py:856
  39.3 28.4 %collective-permute-start.9 = (bf16[108,16,128]{2,1,0:T(8,128)(2,1)S(1)}, bf16[108,16,128]{2,1,0:T(8,128)(2,1)S(1)}, u32[]{:S(2)}, u32[]{:S(2)}) collective-permute-start(bf16[108,16,128]{2,1,0:T(8,128)(2,1)S(1)} %pad_maximum_fusion.11), channel_id=1, source_target_pairs={{0,8},{1,9},{2,10},{3,11},{4,12},{5,13},{6,14},{7,15},{8,0},{9,1},... | collective-permute-start | bytes 1327112 | tf_op jit(solution)/shard_map/ppermute | solution.py:856
  72.5 24.9 %collective-permute-start.15 = (bf16[2048,128]{1,0:T(8,128)(2,1)S(1)}, bf16[2048,128]{1,0:T(8,128)(2,1)S(1)}, u32[]{:S(2)}, u32[]{:S(2)}) collective-permute-start(bf16[2048,128]{1,0:T(8,128)(2,1)S(1)} %pad_maximum_fusion.10), channel_id=1, source_target_pairs={{0,4},{1,5},{2,6},{3,7},{4,0},{5,1},{6,2},{7,3},{8,12},{9,13},{10,... | collective-permute-start | bytes 1572872 | tf_op jit(solution)/shard_map/ppermute | solution.py:856
  74.8 45.2 %collective-permute-start.16 = (bf16[2048,128]{1,0:T(8,128)(2,1)S(1)}, bf16[2048,128]{1,0:T(8,128)(2,1)S(1)}, u32[]{:S(2)}, u32[]{:S(2)}) collective-permute-start(bf16[2048,128]{1,0:T(8,128)(2,1)S(1)} %pad_maximum_fusion.10), channel_id=1, source_target_pairs={{0,6},{1,7},{2,4},{3,5},{4,2},{5,3},{6,0},{7,1},{8,14},{9,15},{10,... | collective-permute-start | bytes 1572872 | tf_op jit(solution)/shard_map/ppermute | solution.py:856
  86.0 37.7 %collective-permute-start.13 = (bf16[324,16,128]{2,1,0:T(8,128)(2,1)S(1)}, bf16[324,16,128]{2,1,0:T(8,128)(2,1)}, u32[]{:S(2)}, u32[]{:S(2)}) collective-permute-start(bf16[324,16,128]{2,1,0:T(8,128)(2,1)S(1)} %pad_maximum_fusion.3), channel_id=1, source_target_pairs={{0,8},{1,9},{2,10},{3,11},{4,12},{5,13},{6,14},{7,15},{8,0},{9,1},... | collective-permute-start | bytes 3981320 | tf_op jit(solution)/shard_map/ppermute | solution.py:856
  86.2 37.5 %collective-permute-start.11 = (bf16[324,16,128]{2,1,0:T(8,128)(2,1)S(1)}, bf16[324,16,128]{2,1,0:T(8,128)(2,1)}, u32[]{:S(2)}, u32[]{:S(2)}) collective-permute-start(bf16[324,16,128]{2,1,0:T(8,128)(2,1)S(1)} %pad_maximum_fusion.2), channel_id=1, source_target_pairs={{0,16},{1,17},{2,18},{3,19},{4,20},{5,21},{6,22},{7,23},{8,24},{9,... | collective-permute-start | bytes 3981320 | tf_op jit(solution)/shard_map/ppermute | solution.py:856
  125.9 27.5 %collective-permute-start.17 = (bf16[216,16,128]{2,1,0:T(8,128)(2,1)S(1)}, bf16[216,16,128]{2,1,0:T(8,128)(2,1)S(1)}, u32[]{:S(2)}, u32[]{:S(2)}) collective-permute-start(bf16[216,16,128]{2,1,0:T(8,128)(2,1)S(1)} %pad_maximum_fusion.5), channel_id=1, source_target_pairs={{0,8},{1,9},{2,10},{3,11},{4,12},{5,13},{6,14},{7,15},{8,0},{9,1},... | collective-permute-start | bytes 2654216 | tf_op jit(solution)/shard_map/ppermute | solution.py:856
  126.0 27.5 %collective-permute-start.18 = (bf16[216,16,128]{2,1,0:T(8,128)(2,1)S(1)}, bf16[216,16,128]{2,1,0:T(8,128)(2,1)S(1)}, u32[]{:S(2)}, u32[]{:S(2)}) collective-permute-start(bf16[216,16,128]{2,1,0:T(8,128)(2,1)S(1)} %pad_maximum_fusion.6), channel_id=1, source_target_pairs={{0,16},{1,17},{2,18},{3,19},{4,20},{5,21},{6,22},{7,23},{8,24},{9,... | collective-permute-start | bytes 2654216 | tf_op jit(solution)/shard_map/ppermute | solution.py:856
  155.1 44.1 %collective-permute-start.26 = (bf16[432,16,128]{2,1,0:T(8,128)(2,1)S(1)}, bf16[432,16,128]{2,1,0:T(8,128)(2,1)}, u32[]{:S(2)}, u32[]{:S(2)}) collective-permute-start(bf16[432,16,128]{2,1,0:T(8,128)(2,1)S(1)} %constant_dynamic-update-slice_fusion.10.refs_4_), channel_id=1, source_target_pairs={{0,1},{1,0},{2,3},{3,2},{4,5},{5,4},{6,7},{7,6},{8,9},{9,8},{10,11... | collective-permute-start | bytes 5308424 | tf_op jit(solution)/shard_map/ppermute | solution.py:856
  157.2 42.0 %collective-permute-start.23 = (bf16[432,16,128]{2,1,0:T(8,128)(2,1)}, bf16[432,16,128]{2,1,0:T(8,128)(2,1)}, u32[]{:S(2)}, u32[]{:S(2)}) collective-permute-start(bf16[432,16,128]{2,1,0:T(8,128)(2,1)} %pad_maximum_fusion.1), channel_id=1, source_target_pairs={{0,8},{1,9},{2,10},{3,11},{4,12},{5,13},{6,14},{7,15},{8,0},{9,1},... | collective-permute-start | bytes 5308424 | tf_op jit(solution)/shard_map/ppermute | solution.py:856
  160.0 39.4 %collective-permute-start.22 = (bf16[432,16,128]{2,1,0:T(8,128)(2,1)}, bf16[432,16,128]{2,1,0:T(8,128)(2,1)S(1)}, u32[]{:S(2)}, u32[]{:S(2)}) collective-permute-start(bf16[432,16,128]{2,1,0:T(8,128)(2,1)} %pad_maximum_fusion), channel_id=1, source_target_pairs={{0,16},{1,17},{2,18},{3,19},{4,20},{5,21},{6,22},{7,23},{8,24},{9,... | collective-permute-start | bytes 5308424 | tf_op jit(solution)/shard_map/ppermute | solution.py:856
  161.5 24.2 %collective-permute-start.24 = (bf16[216,16,128]{2,1,0:T(8,128)(2,1)S(1)}, bf16[216,16,128]{2,1,0:T(8,128)(2,1)S(1)}, u32[]{:S(2)}, u32[]{:S(2)}) collective-permute-start(bf16[216,16,128]{2,1,0:T(8,128)(2,1)S(1)} %copy-done.10), channel_id=1, source_target_pairs={{0,1},{1,0},{2,3},{3,2},{4,5},{5,4},{6,7},{7,6},{8,9},{9,8},{10,11... | collective-permute-start | bytes 2654216 | tf_op jit(solution)/shard_map/ppermute | solution.py:856
  315.1 40.0 %collective-permute-start.32 = (bf16[432,16,128]{2,1,0:T(8,128)(2,1)}, bf16[432,16,128]{2,1,0:T(8,128)(2,1)S(1)}, u32[]{:S(2)}, u32[]{:S(2)}) collective-permute-start(bf16[432,16,128]{2,1,0:T(8,128)(2,1)} %get-tuple-element.293), channel_id=1, source_target_pairs={{0,16},{1,17},{2,18},{3,19},{4,20},{5,21},{6,22},{7,23},{8,24},{9,... | collective-permute-start | bytes 5308424 | tf_op jit(solution)/shard_map/ppermute | solution.py:856
  316.5 39.7 %collective-permute-start.31 = (bf16[432,16,128]{2,1,0:T(8,128)(2,1)}, bf16[432,16,128]{2,1,0:T(8,128)(2,1)S(1)}, u32[]{:S(2)}, u32[]{:S(2)}) collective-permute-start(bf16[432,16,128]{2,1,0:T(8,128)(2,1)} %get-tuple-element.288), channel_id=1, source_target_pairs={{0,8},{1,9},{2,10},{3,11},{4,12},{5,13},{6,14},{7,15},{8,0},{9,1},... | collective-permute-start | bytes 5308424 | tf_op jit(solution)/shard_map/ppermute | solution.py:856
  401.7 43.7 %collective-permute-start.38 = (bf16[432,16,128]{2,1,0:T(8,128)(2,1)}, bf16[432,16,128]{2,1,0:T(8,128)(2,1)}, u32[]{:S(2)}, u32[]{:S(2)}) collective-permute-start(bf16[432,16,128]{2,1,0:T(8,128)(2,1)} %get-tuple-element.354), channel_id=1, source_target_pairs={{0,16},{1,17},{2,18},{3,19},{4,20},{5,21},{6,22},{7,23},{8,24},{9,... | collective-permute-start | bytes 5308424 | tf_op jit(solution)/shard_map/ppermute | solution.py:856
  403.1 42.3 %collective-permute-start.37 = (bf16[432,16,128]{2,1,0:T(8,128)(2,1)}, bf16[432,16,128]{2,1,0:T(8,128)(2,1)}, u32[]{:S(2)}, u32[]{:S(2)}) collective-permute-start(bf16[432,16,128]{2,1,0:T(8,128)(2,1)} %get-tuple-element.349), channel_id=1, source_target_pairs={{0,8},{1,9},{2,10},{3,11},{4,12},{5,13},{6,14},{7,15},{8,0},{9,1},... | collective-permute-start | bytes 5308424 | tf_op jit(solution)/shard_map/ppermute | solution.py:856
  406.9 38.6 %collective-permute-start.41 = (bf16[108,16,128]{2,1,0:T(8,128)(2,1)}, bf16[108,16,128]{2,1,0:T(8,128)(2,1)}, u32[]{:S(2)}, u32[]{:S(2)}) collective-permute-start(bf16[108,16,128]{2,1,0:T(8,128)(2,1)} %pad_maximum_fusion.15), channel_id=1, source_target_pairs={{0,6},{1,7},{2,4},{3,5},{4,2},{5,3},{6,0},{7,1},{8,14},{9,15},{10,... | collective-permute-start | bytes 1327112 | tf_op jit(solution)/shard_map/ppermute | solution.py:856
  470.6 46.0 %collective-permute-start.49 = (bf16[108,16,128]{2,1,0:T(8,128)(2,1)S(1)}, bf16[108,16,128]{2,1,0:T(8,128)(2,1)S(1)}, u32[]{:S(2)}, u32[]{:S(2)}) collective-permute-start(bf16[108,16,128]{2,1,0:T(8,128)(2,1)S(1)} %pad_maximum_fusion.19), channel_id=1, source_target_pairs={{0,6},{1,7},{2,4},{3,5},{4,2},{5,3},{6,0},{7,1},{8,14},{9,15},{10,... | collective-permute-start | bytes 1327112 | tf_op jit(solution)/shard_map/ppermute | solution.py:856
  471.9 44.8 %collective-permute-start.48 = (bf16[108,16,128]{2,1,0:T(8,128)(2,1)S(1)}, bf16[108,16,128]{2,1,0:T(8,128)(2,1)S(1)}, u32[]{:S(2)}, u32[]{:S(2)}) collective-permute-start(bf16[108,16,128]{2,1,0:T(8,128)(2,1)S(1)} %pad_maximum_fusion.18), channel_id=1, source_target_pairs={{0,4},{1,5},{2,6},{3,7},{4,0},{5,1},{6,2},{7,3},{8,12},{9,13},{10,... | collective-permute-start | bytes 1327112 | tf_op jit(solution)/shard_map/ppermute | solution.py:856
  474.0 42.7 %collective-permute-start.47 = (bf16[108,16,128]{2,1,0:T(8,128)(2,1)S(1)}, bf16[108,16,128]{2,1,0:T(8,128)(2,1)S(1)}, u32[]{:S(2)}, u32[]{:S(2)}) collective-permute-start(bf16[108,16,128]{2,1,0:T(8,128)(2,1)S(1)} %pad_maximum_fusion.17), channel_id=1, source_target_pairs={{0,2},{1,3},{2,0},{3,1},{4,6},{5,7},{6,4},{7,5},{8,10},{9,11},{10,... | collective-permute-start | bytes 1327112 | tf_op jit(solution)/shard_map/ppermute | solution.py:856
  478.7 34.2 %collective-permute-start.52 = (bf16[384,128]{1,0:T(8,128)(2,1)S(1)}, bf16[384,128]{1,0:T(8,128)(2,1)S(1)}, u32[]{:S(2)}, u32[]{:S(2)}) collective-permute-start(bf16[384,128]{1,0:T(8,128)(2,1)S(1)} %bitcast.118), channel_id=1, source_target_pairs={{0,1},{1,2},{2,3},{3,4},{4,5},{5,6},{6,7},{7,8},{8,9},{9,10},{10,1... | collective-permute-start | bytes 294920 | tf_op jit(solution)/shard_map/ppermute | solution.py:116
  486.8 26.0 %collective-permute-start.53 = (bf16[288,128]{1,0:T(8,128)(2,1)S(1)}, bf16[288,128]{1,0:T(8,128)(2,1)S(1)}, u32[]{:S(2)}, u32[]{:S(2)}) collective-permute-start(bf16[288,128]{1,0:T(8,128)(2,1)S(1)} %bitcast.122), channel_id=1, source_target_pairs={{1,0},{2,1},{3,2},{4,3},{5,4},{6,5},{7,6},{8,7},{9,8},{10,9},{11,1... | collective-permute-start | bytes 221192 | tf_op jit(solution)/shard_map/ppermute | solution.py:120
  (59 other events, 529.2 us)
